TPU v7x, 32 devices: a whole 2x2x4 slice. The times are simulated.
32 devices in a mesh: dp: 2 (over x), pipe: 4 (over y, core), tensor: 4 (over z).
Axes of the slice: x: 2, y: 2, z: 4, core: 2. Of those that a mesh axis runs over, the one named last changes fastest.
Arguments:
- grad_out: bfloat16 [8, 128, 4096], P(None, 'dp', 'tensor'), may hold values from -6 to 6
- activations: bfloat16 [4, 3, 8, 128, 4096], P('pipe', None, None, 'dp', 'tensor'), may hold values from -6 to 6
- mixing: bfloat16 [4, 3, 32, 128, 128], P('pipe', None, 'tensor'), may hold values from -0.1875 to 0.1875
- proj_tiles: bfloat16 [4, 3, 8, 128, 128], P('pipe'), may hold values from -0.1875 to 0.1875
- proj_blocks: int32 [4, 3, 8], P('pipe'), may hold values from 0 to 31, all different within a row
- section_sizes: int32 [4], replicated, may hold values from 1 to 3, 8 in all
Outputs:
- segment_grads: bfloat16 [4, 8, 128, 4096], P('pipe', None, 'dp', 'tensor')
- sketches: float32 [4, 3, 8, 4096], P('pipe')
Inputs may be any that keep to these rules, and one draw needn't show every extreme that they name: `section_sizes`: each segment holds 1 to 3 layers, 8 in all, some segment exactly 3. `proj_blocks`: the 8 blocks of one slot are distinct.
All inputs are finite; a program needn't handle non-finite values.
Results may differ from a plain program's by a relative error of at most 0.0074.
Values may be sent and summed in bfloat16 or wider, within the bound.
No kernel may reach another device: no remote copies, remote signals or barrier semaphores. Data moves between devices by JAX's collectives and lax.ppermute only.
A program may use at most 64 MiB of HBM per device.

v0:
```python
import math

import jax
import jax.numpy as jnp
from jax import lax
from jax.sharding import PartitionSpec as P


def shifted(x, axis, by):
    peers = lax.axis_size(axis)
    pairs = [(i, i + by) for i in range(peers) if 0 <= i + by < peers]
    return lax.ppermute(x, axis, pairs)


def silu_slope(value):
    sig = jax.nn.sigmoid(value)
    return sig * (1.0 + value * (1.0 - sig))


def shards(grad_out, activations, mixing, proj_tiles, proj_blocks, section_sizes):
    high = lax.Precision.HIGHEST
    segments = lax.axis_size("pipe")
    segment = lax.axis_index("pipe")
    half = lax.axis_index("tensor")
    micro = grad_out.shape[0]
    tokens = grad_out.shape[1]
    local_width = grad_out.shape[2]
    slots = activations.shape[1]
    heads_local = mixing.shape[2]
    head_size = mixing.shape[3]
    rank = proj_tiles.shape[4] // 2
    scale = 1.0 / math.sqrt(tokens * lax.axis_size("dp"))
    live_count = section_sizes[segment]
    owned = heads_local * half + jnp.arange(heads_local, dtype=jnp.int32)
    select = (proj_blocks[0][:, :, None] == owned[None, None, :]).astype(jnp.bfloat16)
    dense = jnp.einsum("kjb,kjcr->kbcr", select, proj_tiles[0], preferred_element_type=jnp.float32)
    dense = dense.astype(jnp.bfloat16).reshape(slots, heads_local * head_size, 2 * rank)
    live_slots = jnp.arange(slots, dtype=jnp.int32) < live_count

    def process(grad, start, width):
        acts = lax.dynamic_slice_in_dim(activations[0], start, width, 1)
        act_parts = [None] * slots
        delta_parts = [None] * slots
        for slot in range(slots - 1, -1, -1):
            flat_act = acts[slot].reshape(width * tokens, local_width)
            heads_in = acts[slot].reshape(width, tokens, heads_local, head_size)
            pre = jnp.einsum(
                "mthc,hcd->mthd", heads_in, mixing[0, slot], preferred_element_type=jnp.float32
            )
            grad_heads = grad.reshape(width, tokens, heads_local, head_size).astype(jnp.float32)
            delta = (grad_heads * silu_slope(pre)).astype(jnp.bfloat16)
            back = jnp.einsum(
                "mthd,hcd->mthc", delta, mixing[0, slot], preferred_element_type=jnp.float32
            )
            moved = (grad_heads + back).reshape(width, tokens, local_width).astype(jnp.bfloat16)
            grad = jnp.where(slot < live_count, moved, grad)
            act_parts[slot] = jnp.dot(
                flat_act, dense[slot, :, :rank], preferred_element_type=jnp.float32
            )
            delta_parts[slot] = jnp.dot(
                delta.reshape(width * tokens, local_width),
                dense[slot, :, rank:],
                preferred_element_type=jnp.float32,
            )
        act_proj, grad_proj = lax.psum((jnp.stack(act_parts), jnp.stack(delta_parts)), "tensor")
        act_proj = act_proj.reshape(slots, width, tokens, rank)
        grad_proj = grad_proj.reshape(slots, width, tokens, rank)
        sketch = jnp.einsum("kmtr,kmts->kmrs", grad_proj, act_proj, precision=high) * scale
        sketch = jnp.where(live_slots[:, None, None, None], sketch, 0.0).reshape(
            slots, width, rank * rank
        )
        return (grad, sketch)

    width = 2
    groups = micro // width
    turns = groups + segments - 1

    def turn(step, carry):
        incoming, segment_out, sketches = carry
        group = step - (segments - 1 - segment)
        valid = jnp.logical_and(group >= 0, group < groups)
        start = jnp.clip(group, 0, groups - 1) * width
        top = lax.dynamic_slice_in_dim(grad_out, start, width, 0)
        grad = jnp.where(segment == segments - 1, top, incoming)
        grad, sketch = process(grad, start, width)
        sketch = lax.psum(sketch, "dp")
        old_out = lax.dynamic_slice_in_dim(segment_out, start, width, 0)
        segment_out = lax.dynamic_update_slice_in_dim(
            segment_out, jnp.where(valid, grad, old_out), start, 0
        )
        old_sketch = lax.dynamic_slice_in_dim(sketches, start, width, 1)
        sketches = lax.dynamic_update_slice_in_dim(
            sketches, jnp.where(valid, sketch, old_sketch), start, 1
        )
        incoming = shifted(grad, "pipe", -1)
        return (incoming, segment_out, sketches)

    start_carry = (
        jnp.zeros((width, tokens, local_width), jnp.bfloat16),
        jnp.zeros_like(grad_out),
        jnp.zeros((slots, micro, rank * rank), jnp.float32),
    )
    incoming, segment_out, sketches = lax.fori_loop(0, turns, turn, start_carry)
    return (segment_out[None], sketches[None])


def solution(mesh):
    return jax.shard_map(
        shards,
        mesh=mesh,
        in_specs=(
            P(None, "dp", "tensor"),
            P("pipe", None, None, "dp", "tensor"),
            P("pipe", None, "tensor", None, None),
            P("pipe", None, None, None, None),
            P("pipe", None, None),
            P(),
        ),
        out_specs=(P("pipe", None, "dp", "tensor"), P("pipe", None, None, None)),
        check_vma=False,
    )
```

profile of v0, /device:TPU:0, one launch (start us, length us, event | category | flops | bytes accessed | tf_op | source)
XLA Modules:
  0.0 546.9 jit_solution(14757082469023561249)
XLA Ops:
  7.2 1.4 dynamic_slice.35
  14.0 526.4 %while.20 = (s32[]{:T(128)}, bf16[2,64,1024]{2,1,0:T(8,128)(2,1)S(1)}, bf16[8,64,1024]{2,1,0:T(8,128)(2,1)}, f32[3,8,4096]{2,1,0:T(8,128)}, pred[]{:T(512)}, /*i...) while((s32[]{:T(128)}, ...), condition=%wide.region_4.5_spmd.clone, body=%wide.region_0.4_spmd.clone.sunk | while | flops 326877184 | bytes 25102308 | solution.py:103
  16.2 1.3 fusion.120
  19.0 1.3 fusion.122
  29.0 38.0 %all-reduce.6.cloned.1.call-done = (f32[3,2,64,64]{2,3,1,0:T(8,128)}, f32[3,2,64,64]{3,2,1,0:T(8,128)}) async-done(((f32[3,2,64,64]{2,3,1,0:T(8,128)}, f32[3,2,64,64]{3,2,1,0:T(8,128)}), (f32[3,2,64,64]{2,3,1,0:T(8,128)}, f32[3,2,64,64]{3,2,1,0:T(8,128)})) %all-reduce.6.cloned.1.call-update) | async-done | bytes 196624 | tf_op jit(solution)/shard_map/while/body/eval_jaxpr/psum | solution.py:65
  67.0 1.3 fusion.126
  69.1 1.8 select_dynamic-update-slice_fusion.4
  72.2 17.6 %all-reduce.8.cloned.1.call-done = f32[3,2,4096]{2,1,0:T(2,128)} async-done(((f32[3,2,4096]{2,1,0:T(2,128)}), f32[3,2,4096]{2,1,0:T(2,128)}) %all-reduce.8.cloned.1.call-update) | async-done | bytes 98320 | tf_op jit(solution)/shard_map/while/body/eval_jaxpr/psum | solution.py:86
  89.8 1.7 select_dynamic-update-slice_fusion.5
  93.8 1.3 fusion.120
  96.6 1.3 fusion.122
  106.6 35.3 %all-reduce.6.cloned.1.call-done = (f32[3,2,64,64]{2,3,1,0:T(8,128)}, f32[3,2,64,64]{3,2,1,0:T(8,128)}) async-done(((f32[3,2,64,64]{2,3,1,0:T(8,128)}, f32[3,2,64,64]{3,2,1,0:T(8,128)}), (f32[3,2,64,64]{2,3,1,0:T(8,128)}, f32[3,2,64,64]{3,2,1,0:T(8,128)})) %all-reduce.6.cloned.1.call-update) | async-done | bytes 196624 | tf_op jit(solution)/shard_map/while/body/eval_jaxpr/psum | solution.py:65
  141.8 1.3 fusion.126
  144.0 1.8 select_dynamic-update-slice_fusion.4
  147.0 17.6 %all-reduce.8.cloned.1.call-done = f32[3,2,4096]{2,1,0:T(2,128)} async-done(((f32[3,2,4096]{2,1,0:T(2,128)}), f32[3,2,4096]{2,1,0:T(2,128)}) %all-reduce.8.cloned.1.call-update) | async-done | bytes 98320 | tf_op jit(solution)/shard_map/while/body/eval_jaxpr/psum | solution.py:86
  164.6 1.7 select_dynamic-update-slice_fusion.5
  171.4 1.3 fusion.122
  181.4 35.3 %all-reduce.6.cloned.1.call-done = (f32[3,2,64,64]{2,3,1,0:T(8,128)}, f32[3,2,64,64]{3,2,1,0:T(8,128)}) async-done(((f32[3,2,64,64]{2,3,1,0:T(8,128)}, f32[3,2,64,64]{3,2,1,0:T(8,128)}), (f32[3,2,64,64]{2,3,1,0:T(8,128)}, f32[3,2,64,64]{3,2,1,0:T(8,128)})) %all-reduce.6.cloned.1.call-update) | async-done | bytes 196624 | tf_op jit(solution)/shard_map/while/body/eval_jaxpr/psum | solution.py:65
  216.6 1.3 fusion.126
  218.8 1.8 select_dynamic-update-slice_fusion.4
  221.8 17.6 %all-reduce.8.cloned.1.call-done = f32[3,2,4096]{2,1,0:T(2,128)} async-done(((f32[3,2,4096]{2,1,0:T(2,128)}), f32[3,2,4096]{2,1,0:T(2,128)}) %all-reduce.8.cloned.1.call-update) | async-done | bytes 98320 | tf_op jit(solution)/shard_map/while/body/eval_jaxpr/psum | solution.py:86
  239.4 1.7 select_dynamic-update-slice_fusion.5
  243.4 1.3 fusion.120
  246.2 1.3 fusion.122
  256.2 35.2 %all-reduce.6.cloned.1.call-done = (f32[3,2,64,64]{2,3,1,0:T(8,128)}, f32[3,2,64,64]{3,2,1,0:T(8,128)}) async-done(((f32[3,2,64,64]{2,3,1,0:T(8,128)}, f32[3,2,64,64]{3,2,1,0:T(8,128)}), (f32[3,2,64,64]{2,3,1,0:T(8,128)}, f32[3,2,64,64]{3,2,1,0:T(8,128)})) %all-reduce.6.cloned.1.call-update) | async-done | bytes 196624 | tf_op jit(solution)/shard_map/while/body/eval_jaxpr/psum | solution.py:65
  291.4 1.3 fusion.126
  293.5 1.8 select_dynamic-update-slice_fusion.4
  296.6 17.6 %all-reduce.8.cloned.1.call-done = f32[3,2,4096]{2,1,0:T(2,128)} async-done(((f32[3,2,4096]{2,1,0:T(2,128)}), f32[3,2,4096]{2,1,0:T(2,128)}) %all-reduce.8.cloned.1.call-update) | async-done | bytes 98320 | tf_op jit(solution)/shard_map/while/body/eval_jaxpr/psum | solution.py:86
  314.3 1.7 select_dynamic-update-slice_fusion.5
  321.0 1.3 fusion.122
  331.0 35.3 %all-reduce.6.cloned.1.call-done = (f32[3,2,64,64]{2,3,1,0:T(8,128)}, f32[3,2,64,64]{3,2,1,0:T(8,128)}) async-done(((f32[3,2,64,64]{2,3,1,0:T(8,128)}, f32[3,2,64,64]{3,2,1,0:T(8,128)}), (f32[3,2,64,64]{2,3,1,0:T(8,128)}, f32[3,2,64,64]{3,2,1,0:T(8,128)})) %all-reduce.6.cloned.1.call-update) | async-done | bytes 196624 | tf_op jit(solution)/shard_map/while/body/eval_jaxpr/psum | solution.py:65
  366.3 1.3 fusion.126
  368.4 1.8 select_dynamic-update-slice_fusion.4
  371.5 17.6 %all-reduce.8.cloned.1.call-done = f32[3,2,4096]{2,1,0:T(2,128)} async-done(((f32[3,2,4096]{2,1,0:T(2,128)}), f32[3,2,4096]{2,1,0:T(2,128)}) %all-reduce.8.cloned.1.call-update) | async-done | bytes 98320 | tf_op jit(solution)/shard_map/while/body/eval_jaxpr/psum | solution.py:86
  389.1 1.7 select_dynamic-update-slice_fusion.5
  393.0 1.3 fusion.120
  395.8 1.3 fusion.122
  405.8 35.2 %all-reduce.6.cloned.1.call-done = (f32[3,2,64,64]{2,3,1,0:T(8,128)}, f32[3,2,64,64]{3,2,1,0:T(8,128)}) async-done(((f32[3,2,64,64]{2,3,1,0:T(8,128)}, f32[3,2,64,64]{3,2,1,0:T(8,128)}), (f32[3,2,64,64]{2,3,1,0:T(8,128)}, f32[3,2,64,64]{3,2,1,0:T(8,128)})) %all-reduce.6.cloned.1.call-update) | async-done | bytes 196624 | tf_op jit(solution)/shard_map/while/body/eval_jaxpr/psum | solution.py:65
  441.1 1.3 fusion.126
  443.2 1.8 select_dynamic-update-slice_fusion.4
  446.3 17.6 %all-reduce.8.cloned.1.call-done = f32[3,2,4096]{2,1,0:T(2,128)} async-done(((f32[3,2,4096]{2,1,0:T(2,128)}), f32[3,2,4096]{2,1,0:T(2,128)}) %all-reduce.8.cloned.1.call-update) | async-done | bytes 98320 | tf_op jit(solution)/shard_map/while/body/eval_jaxpr/psum | solution.py:86
  463.8 1.7 select_dynamic-update-slice_fusion.5
  470.6 1.3 fusion.122
  480.6 35.3 %all-reduce.6.cloned.1.call-done = (f32[3,2,64,64]{2,3,1,0:T(8,128)}, f32[3,2,64,64]{3,2,1,0:T(8,128)}) async-done(((f32[3,2,64,64]{2,3,1,0:T(8,128)}, f32[3,2,64,64]{3,2,1,0:T(8,128)}), (f32[3,2,64,64]{2,3,1,0:T(8,128)}, f32[3,2,64,64]{3,2,1,0:T(8,128)})) %all-reduce.6.cloned.1.call-update) | async-done | bytes 196624 | tf_op jit(solution)/shard_map/while/body/eval_jaxpr/psum | solution.py:65
  515.9 1.3 fusion.126
  518.0 1.8 select_dynamic-update-slice_fusion.4
  521.1 17.6 %all-reduce.8.cloned.1.call-done = f32[3,2,4096]{2,1,0:T(2,128)} async-done(((f32[3,2,4096]{2,1,0:T(2,128)}), f32[3,2,4096]{2,1,0:T(2,128)}) %all-reduce.8.cloned.1.call-update) | async-done | bytes 98320 | tf_op jit(solution)/shard_map/while/body/eval_jaxpr/psum | solution.py:86
  538.6 1.7 select_dynamic-update-slice_fusion.5
  (236 shorter events, 107.3 us)
Async XLA Ops:
  7.2 3.4 copy-start
  14.0 53.0 %all-reduce.6.cloned.1.call-start = ((), (), s32[]{:S(2)}) async-start(), calls=%async_computation | async-start | bytes 786432 | tf_op jit(solution)/shard_map/while/body/eval_jaxpr/psum | solution.py:65
  27.0 62.8 %all-reduce.8.cloned.1.call-start = ((), (), s32[]{:S(2)}) async-start(), calls=%async_computation.1 | async-start | bytes 196608 | tf_op jit(solution)/shard_map/while/body/eval_jaxpr/psum | solution.py:86
  70.9 20.6 %collective-permute-start = (bf16[2,64,1024]{2,1,0:T(8,128)(2,1)S(1)}, bf16[2,64,1024]{2,1,0:T(8,128)(2,1)S(1)}, u32[]{:S(2)}, u32[]{:S(2)}) collective-permute-start(bf16[2,64,1024]{2,1,0:T(8,128)(2,1)S(1)} %get-tuple-element.449), channel_id=1, source_target_pairs={{4,0},{8,4},{12,8},{5,1},{9,5},{13,9},{6,2},{10,6},{14,10},{7,3},{... | collective-permute-start | bytes 786440 | tf_op jit(solution)/shard_map/while/body/eval_jaxpr/ppermute | solution.py:12
  91.5 50.3 %all-reduce.6.cloned.1.call-start = ((), (), s32[]{:S(2)}) async-start(), calls=%async_computation | async-start | bytes 786432 | tf_op jit(solution)/shard_map/while/body/eval_jaxpr/psum | solution.py:65
  104.6 60.0 %all-reduce.8.cloned.1.call-start = ((), (), s32[]{:S(2)}) async-start(), calls=%async_computation.1 | async-start | bytes 196608 | tf_op jit(solution)/shard_map/while/body/eval_jaxpr/psum | solution.py:86
  145.8 20.6 %collective-permute-start = (bf16[2,64,1024]{2,1,0:T(8,128)(2,1)S(1)}, bf16[2,64,1024]{2,1,0:T(8,128)(2,1)S(1)}, u32[]{:S(2)}, u32[]{:S(2)}) collective-permute-start(bf16[2,64,1024]{2,1,0:T(8,128)(2,1)S(1)} %get-tuple-element.449), channel_id=1, source_target_pairs={{4,0},{8,4},{12,8},{5,1},{9,5},{13,9},{6,2},{10,6},{14,10},{7,3},{... | collective-permute-start | bytes 786440 | tf_op jit(solution)/shard_map/while/body/eval_jaxpr/ppermute | solution.py:12
  166.3 50.3 %all-reduce.6.cloned.1.call-start = ((), (), s32[]{:S(2)}) async-start(), calls=%async_computation | async-start | bytes 786432 | tf_op jit(solution)/shard_map/while/body/eval_jaxpr/psum | solution.py:65
  179.4 60.1 %all-reduce.8.cloned.1.call-start = ((), (), s32[]{:S(2)}) async-start(), calls=%async_computation.1 | async-start | bytes 196608 | tf_op jit(solution)/shard_map/while/body/eval_jaxpr/psum | solution.py:86
  220.6 20.5 %collective-permute-start = (bf16[2,64,1024]{2,1,0:T(8,128)(2,1)S(1)}, bf16[2,64,1024]{2,1,0:T(8,128)(2,1)S(1)}, u32[]{:S(2)}, u32[]{:S(2)}) collective-permute-start(bf16[2,64,1024]{2,1,0:T(8,128)(2,1)S(1)} %get-tuple-element.449), channel_id=1, source_target_pairs={{4,0},{8,4},{12,8},{5,1},{9,5},{13,9},{6,2},{10,6},{14,10},{7,3},{... | collective-permute-start | bytes 786440 | tf_op jit(solution)/shard_map/while/body/eval_jaxpr/ppermute | solution.py:12
  241.1 50.3 %all-reduce.6.cloned.1.call-start = ((), (), s32[]{:S(2)}) async-start(), calls=%async_computation | async-start | bytes 786432 | tf_op jit(solution)/shard_map/while/body/eval_jaxpr/psum | solution.py:65
  254.2 60.1 %all-reduce.8.cloned.1.call-start = ((), (), s32[]{:S(2)}) async-start(), calls=%async_computation.1 | async-start | bytes 196608 | tf_op jit(solution)/shard_map/while/body/eval_jaxpr/psum | solution.py:86
  295.3 20.6 %collective-permute-start = (bf16[2,64,1024]{2,1,0:T(8,128)(2,1)S(1)}, bf16[2,64,1024]{2,1,0:T(8,128)(2,1)S(1)}, u32[]{:S(2)}, u32[]{:S(2)}) collective-permute-start(bf16[2,64,1024]{2,1,0:T(8,128)(2,1)S(1)} %get-tuple-element.449), channel_id=1, source_target_pairs={{4,0},{8,4},{12,8},{5,1},{9,5},{13,9},{6,2},{10,6},{14,10},{7,3},{... | collective-permute-start | bytes 786440 | tf_op jit(solution)/shard_map/while/body/eval_jaxpr/ppermute | solution.py:12
  316.0 50.3 %all-reduce.6.cloned.1.call-start = ((), (), s32[]{:S(2)}) async-start(), calls=%async_computation | async-start | bytes 786432 | tf_op jit(solution)/shard_map/while/body/eval_jaxpr/psum | solution.py:65
  329.0 60.0 %all-reduce.8.cloned.1.call-start = ((), (), s32[]{:S(2)}) async-start(), calls=%async_computation.1 | async-start | bytes 196608 | tf_op jit(solution)/shard_map/while/body/eval_jaxpr/psum | solution.py:86
  370.2 20.6 %collective-permute-start = (bf16[2,64,1024]{2,1,0:T(8,128)(2,1)S(1)}, bf16[2,64,1024]{2,1,0:T(8,128)(2,1)S(1)}, u32[]{:S(2)}, u32[]{:S(2)}) collective-permute-start(bf16[2,64,1024]{2,1,0:T(8,128)(2,1)S(1)} %get-tuple-element.449), channel_id=1, source_target_pairs={{4,0},{8,4},{12,8},{5,1},{9,5},{13,9},{6,2},{10,6},{14,10},{7,3},{... | collective-permute-start | bytes 786440 | tf_op jit(solution)/shard_map/while/body/eval_jaxpr/ppermute | solution.py:12
  390.8 50.3 %all-reduce.6.cloned.1.call-start = ((), (), s32[]{:S(2)}) async-start(), calls=%async_computation | async-start | bytes 786432 | tf_op jit(solution)/shard_map/while/body/eval_jaxpr/psum | solution.py:65
  403.8 60.0 %all-reduce.8.cloned.1.call-start = ((), (), s32[]{:S(2)}) async-start(), calls=%async_computation.1 | async-start | bytes 196608 | tf_op jit(solution)/shard_map/while/body/eval_jaxpr/psum | solution.py:86
  445.0 20.6 %collective-permute-start = (bf16[2,64,1024]{2,1,0:T(8,128)(2,1)S(1)}, bf16[2,64,1024]{2,1,0:T(8,128)(2,1)S(1)}, u32[]{:S(2)}, u32[]{:S(2)}) collective-permute-start(bf16[2,64,1024]{2,1,0:T(8,128)(2,1)S(1)} %get-tuple-element.449), channel_id=1, source_target_pairs={{4,0},{8,4},{12,8},{5,1},{9,5},{13,9},{6,2},{10,6},{14,10},{7,3},{... | collective-permute-start | bytes 786440 | tf_op jit(solution)/shard_map/while/body/eval_jaxpr/ppermute | solution.py:12
  465.6 50.3 %all-reduce.6.cloned.1.call-start = ((), (), s32[]{:S(2)}) async-start(), calls=%async_computation | async-start | bytes 786432 | tf_op jit(solution)/shard_map/while/body/eval_jaxpr/psum | solution.py:65
  478.6 60.0 %all-reduce.8.cloned.1.call-start = ((), (), s32[]{:S(2)}) async-start(), calls=%async_computation.1 | async-start | bytes 196608 | tf_op jit(solution)/shard_map/while/body/eval_jaxpr/psum | solution.py:86
  519.8 20.6 %collective-permute-start = (bf16[2,64,1024]{2,1,0:T(8,128)(2,1)S(1)}, bf16[2,64,1024]{2,1,0:T(8,128)(2,1)S(1)}, u32[]{:S(2)}, u32[]{:S(2)}) collective-permute-start(bf16[2,64,1024]{2,1,0:T(8,128)(2,1)S(1)} %get-tuple-element.449), channel_id=1, source_target_pairs={{4,0},{8,4},{12,8},{5,1},{9,5},{13,9},{6,2},{10,6},{14,10},{7,3},{... | collective-permute-start | bytes 786440 | tf_op jit(solution)/shard_map/while/body/eval_jaxpr/ppermute | solution.py:12
Sparse Core Ops, SparseCore 0:
  27.1 39.7 all-reduce.5
  69.3 20.4 all-reduce.7
  104.7 37.0 all-reduce.5
  144.1 20.4 all-reduce.7
  179.5 37.1 all-reduce.5
  218.9 20.4 all-reduce.7
  254.3 37.0 all-reduce.5
  293.7 20.4 all-reduce.7
  329.2 37.0 all-reduce.5
  368.5 20.4 all-reduce.7
  403.9 37.0 all-reduce.5
  443.3 20.4 all-reduce.7
  478.7 37.0 all-reduce.5
  518.1 20.4 all-reduce.7
where the time goes:
time: 550 us; the launch traced here: 547 us
  waiting for transfers between devices  373 us (68%)
  matrix products  76.6 us (14%)
  other arithmetic  36.9 us (7%)
  local copies, waits for them, and re-layouts  33.8 us (6%)
  between operations  15.8 us (3%)
  starting transfers between devices  9.27 us (2%)
    psum x7, waiting for transfers between devices, process(): lax.psum((jnp.stack(act_parts), jnp.stack(delta_parts)), 'tensor')  249 us
    psum x7, waiting for transfers between devices, turn(): sketch = lax.psum(sketch, 'dp')  123 us
    dot_general x21, matrix products, process(): jnp.einsum('mthc,hcd->mthd', heads_in, mixing[0, slot], preferred_element...  27.5 us
    dot_general x21, matrix products, process(): jnp.einsum('mthd,hcd->mthc', delta, mixing[0, slot], preferred_element_ty...  26.3 us
    dynamic_update_slice x7, other arithmetic, turn(): lax.dynamic_update_slice_in_dim(segment_out, jnp.where(valid, grad, old_o...  12.5 us
    dynamic_update_slice x7, other arithmetic, turn(): lax.dynamic_update_slice_in_dim(sketches, jnp.where(valid, sketch, old_sk...  11.9 us
  transfers between devices with their start and end apart: 21, of which 14 were waited for; matrix products, arithmetic and copies ran while one was open for 7% of the time, Pallas kernels for 0%

commit v1 on v0

v1 whole, which is shorter than its diff:
```python
import functools
import math

import jax
import jax.numpy as jnp
from jax import lax
from jax.experimental import pallas as pl
from jax.experimental.pallas import tpu as pltpu
from jax.sharding import PartitionSpec as P

F32 = jnp.float32
BF16 = jnp.bfloat16
VMEM = pl.BlockSpec(memory_space=pltpu.VMEM)
SMEM = pl.BlockSpec(memory_space=pltpu.SMEM)
PARAMS = pltpu.CompilerParams(vmem_limit_bytes=48 * 1024 * 1024)


def silu_slope(value):
    sig = 0.5 + 0.5 * jnp.tanh(0.5 * value)
    return sig * (1.0 + value * (1.0 - sig))


def left_lanes(shape, rank):
    return lax.broadcasted_iota(jnp.int32, shape, len(shape) - 1) < rank


def prep_kernel(place, blocks, tiles, acts, dense_g, act_sums, dense_a):
    slots, picks, head_size, both = tiles.shape
    rank = both // 2
    micro = acts.shape[1]
    heads = dense_g.shape[1] // head_size
    row = lax.broadcasted_iota(jnp.int32, (both, both), 0)
    col = lax.broadcasted_iota(jnp.int32, (both, both), 1)
    twice = (row == col % rank).astype(BF16)
    order = rank + jnp.where(col < rank // 2, 2 * col, 2 * col - rank + 1)
    split = jnp.logical_and(row == order, col < rank).astype(BF16)
    dense_a[...] = jnp.zeros_like(dense_a)
    dense_g[...] = jnp.zeros_like(dense_g)
    for k in range(slots):
        for j in range(picks):
            own = blocks[k, j] - place[0] * heads

            @pl.when(jnp.logical_and(own >= 0, own < heads))
            def _():
                rows = pl.ds(pl.multiple_of(own * head_size, head_size), head_size)
                tile = tiles[k, j]
                dense_a[k, rows, :] = jnp.dot(tile, twice, preferred_element_type=F32).astype(BF16)
                dense_g[k, rows, :] = jnp.dot(tile, split, preferred_element_type=F32).astype(BF16)

    half = micro // 2
    tokens = acts.shape[2]

    def project(k, _):
        first = acts[k, :half].reshape(half * tokens, -1)
        second = acts[k, half:].reshape(half * tokens, -1)
        one = jnp.dot(first, dense_a[k], preferred_element_type=F32)
        two = jnp.dot(second, dense_a[k], preferred_element_type=F32)
        act_sums[k] = jnp.where(left_lanes(one.shape, rank), one, two).astype(BF16)
        return 0

    lax.fori_loop(0, slots, project, 0)


def chain_kernel(step, place, *refs, sources, top):
    refs = list(refs)
    odd_in = refs.pop(0) if "odd" in sources else None
    even_in = refs.pop(0) if "even" in sources else None
    acts, mixing, grad, deltas = refs
    chunk, tokens, width = grad.shape
    heads, head_size = mixing.shape[1], mixing.shape[2]
    rows = chunk * tokens
    live, odd, active = place[1], place[2], place[3]
    at = (step - 1 + odd) * chunk

    def run():
        def slot(i, _):
            k = live - 1 - i
            for h in range(heads):
                lanes = slice(h * head_size, (h + 1) * head_size)
                act = acts[k, pl.ds(at, chunk), :, lanes].reshape(rows, head_size)
                weight = mixing[k, h]
                pre = jnp.dot(act, weight, preferred_element_type=F32)
                g = grad[:, :, lanes].reshape(rows, head_size).astype(F32)
                delta = (g * silu_slope(pre)).astype(BF16)
                back = lax.dot_general(delta, weight, (((1,), (1,)), ((), ())), preferred_element_type=F32)
                grad[:, :, lanes] = (g + back).astype(BF16).reshape(chunk, tokens, head_size)
                deltas[k, :, :, lanes] = delta.reshape(chunk, tokens, head_size)
            return 0

        lax.fori_loop(0, live, slot, 0)

    if odd_in is not None:

        @pl.when(jnp.logical_and(active == 1, odd == 1))
        def _():
            if top:
                grad[...] = odd_in[step * chunk : (step + 1) * chunk]
            else:
                grad[...] = odd_in[...]

    if even_in is not None:

        @pl.when(jnp.logical_and(active == 1, odd == 0))
        def _():
            grad[...] = even_in[...]

    if odd_in is None:
        wanted = jnp.logical_and(active == 1, odd == 0)
    elif even_in is None:
        wanted = jnp.logical_and(active == 1, odd == 1)
    else:
        wanted = active == 1

    pl.when(wanted)(run)


def sketch_kernel(place, *refs, count, pairs, scale):
    deltas = [refs[p * (count + 1) : (p + 1) * (count + 1)] for p in range(pairs)]
    dense_g, act_sums, out = refs[pairs * (count + 1) :]
    slots, chunk, tokens, width = deltas[0][0].shape
    both = dense_g.shape[2]
    rank = both // 2
    micro = out.shape[1]
    half = micro // 2
    live, odd, pair = place[1], place[2], place[4]

    def one(ref, c):
        for k in range(slots):

            @pl.when(k < live)
            def _():
                flat = ref[k].reshape(chunk * tokens, width)
                proj = jnp.dot(flat, dense_g[k], preferred_element_type=F32)
                for i in range(chunk):
                    m = c * chunk + i
                    rows = slice((m % half) * tokens, (m % half + 1) * tokens)
                    act = act_sums[k, rows, :]
                    other = pltpu.roll(act, rank, 1)
                    left = left_lanes(act.shape, rank)
                    act = jnp.where(left, act, other) if m < half else jnp.where(left, other, act)
                    full = lax.dot_general(
                        proj[i * tokens : (i + 1) * tokens],
                        act,
                        (((0,), (0,)), ((), ())),
                        precision=lax.Precision.HIGHEST,
                        preferred_element_type=F32,
                    )
                    even, uneven = full[: rank // 2], full[rank // 2 : rank]
                    res = jnp.where(left_lanes(even.shape, rank), even, uneven) * scale
                    out[k, m] = res.astype(BF16)

            @pl.when(k >= live)
            def _():
                out[k, c * chunk : (c + 1) * chunk] = jnp.zeros((chunk, rank // 2, both), BF16)

    for c in range(count):
        for p in range(pairs):
            for parity in (0, 1):

                @pl.when(jnp.logical_and(pair == p, odd == parity))
                def _():
                    one(deltas[p][c + 1 - parity], c)


def swap_sum(x, axis, by):
    peers = lax.axis_size(axis)
    other = lax.ppermute(x, axis, [(i, i ^ by) for i in range(peers)])
    return x.astype(F32) + other.astype(F32)


def all_sum(x, axes):
    x = x.astype(BF16)
    total = x.astype(F32)
    for axis in axes:
        peers = lax.axis_size(axis)
        if peers & (peers - 1):
            total = lax.psum(total, axis)
        else:
            by = 1
            while by < peers:
                total = swap_sum(total.astype(BF16), axis, by)
                by *= 2
    return total


def shards(grad_out, activations, mixing, proj_tiles, proj_blocks, section_sizes):
    sections = lax.axis_size("pipe")
    section = lax.axis_index("pipe")
    micro, tokens, width = grad_out.shape
    slots = activations.shape[1]
    head_size = mixing.shape[3]
    rank = proj_tiles.shape[4] // 2
    scale = 1.0 / math.sqrt(tokens * lax.axis_size("dp"))
    pairs = sections // 2
    count = 4
    chunk = micro // count
    acts, mix = activations[0], mixing[0]
    odd = section % 2
    pair = section // 2
    live = section_sizes[section]
    index = lax.axis_index("tensor")

    def place(p):
        here = (pair == pairs - 1 - p).astype(jnp.int32)
        return jnp.stack([index, live, odd, here, pairs - 1 - pair]).astype(jnp.int32)

    places = [place(p) for p in range(pairs)]
    dense_g, act_part = pl.pallas_call(
        prep_kernel,
        out_shape=(
            jax.ShapeDtypeStruct((slots, width, 2 * rank), BF16),
            jax.ShapeDtypeStruct((slots, micro // 2 * tokens, 2 * rank), BF16),
        ),
        in_specs=[SMEM, SMEM, VMEM, VMEM],
        out_specs=(VMEM, VMEM),
        scratch_shapes=[pltpu.VMEM((slots, width, 2 * rank), BF16)],
        compiler_params=PARAMS,
        name="prep",
    )(places[0], proj_blocks[0], proj_tiles[0], acts)
    act_sums = all_sum(act_part, ("tensor",))

    swap = [(i, i ^ 1) for i in range(sections)]
    from_above = [grad_out] * count
    all_deltas, all_grads = [], []
    for p in range(pairs):
        deltas, grads, below = [], [], []
        even_in = None
        for step in range(count + 1):
            odd_in = from_above[step] if step < count else None
            sources = [n for n, v in (("odd", odd_in), ("even", even_in)) if v is not None]
            ins = [v for v in (odd_in, even_in) if v is not None]
            grad, delta = pl.pallas_call(
                functools.partial(chain_kernel, step, sources=sources, top=p == 0),
                out_shape=(
                    jax.ShapeDtypeStruct((chunk, tokens, width), BF16),
                    jax.ShapeDtypeStruct((slots, chunk, tokens, width), BF16),
                ),
                in_specs=[SMEM] + [VMEM] * (len(ins) + 2),
                out_specs=(VMEM, VMEM),
                compiler_params=PARAMS,
                name="chain",
            )(places[p], *ins, acts, mix)
            if step < count:
                even_in = lax.ppermute(grad, "pipe", swap)
            if step > 0 and p + 1 < pairs:
                source = sections - 2 - 2 * p
                below.append(lax.ppermute(grad, "pipe", [(source, source - 1)]))
            grads.append(grad)
            deltas.append(delta)
        from_above = below
        all_deltas += deltas
        all_grads.append(grads)

    sketch = pl.pallas_call(
        functools.partial(sketch_kernel, count=count, pairs=pairs, scale=scale),
        out_shape=jax.ShapeDtypeStruct((slots, micro, rank // 2, 2 * rank), BF16),
        in_specs=[SMEM] + [VMEM] * (len(all_deltas) + 2),
        out_specs=VMEM,
        compiler_params=PARAMS,
        name="sketch",
    )(places[0], *all_deltas, dense_g, act_sums)
    sketch = all_sum(sketch, ("dp", "tensor")).reshape(slots, micro, rank * rank)

    picked = []
    for step in range(count + 1):
        value = all_grads[0][step]
        for p in range(1, pairs):
            value = jnp.where(pair == pairs - 1 - p, all_grads[p][step], value)
        picked.append(value)
    segment_out = jnp.concatenate([jnp.where(odd == 1, picked[c], picked[c + 1]) for c in range(count)])
    return (segment_out[None], sketch[None])


def solution(mesh):
    return jax.shard_map(
        shards,
        mesh=mesh,
        in_specs=(
            P(None, "dp", "tensor"),
            P("pipe", None, None, "dp", "tensor"),
            P("pipe", None, "tensor", None, None),
            P("pipe", None, None, None, None),
            P("pipe", None, None),
            P(),
        ),
        out_specs=(P("pipe", None, "dp", "tensor"), P("pipe", None, None, None)),
        check_vma=False,
    )
```

time: 550 us -> 98.1 us (0.18)
  the two profiles are of different devices: /device:TPU:0 before, /device:TPU:5 now
where the time goes in v1:
time: 98.1 us; the launch traced here: 98 us
  Pallas kernels  32.8 us (33%)
  waiting for transfers between devices  29.6 us (30%)
  local copies, waits for them, and re-layouts  16.5 us (17%)
  starting transfers between devices  15.6 us (16%)
  other arithmetic  2.52 us (3%)
  between operations  1.03 us (1%)
    ppermute x5, waiting for transfers between devices, swap_sum(): other = lax.ppermute(x, axis, [(i, i ^ by) for i in range(peers)])  27.1 us
    pallas_call x10, Pallas kernels, shards(): pl.pallas_call(functools.partial(chain_kernel, step, sources=sources, top...  21.5 us
    unnamed x53, local copies, waits for them, and re-layouts  13.1 us
    pallas_call x1, Pallas kernels, shards(): pl.pallas_call(functools.partial(sketch_kernel, count=count, pairs=pairs,...  8.31 us
    ppermute x8, starting transfers between devices, shards(): even_in = lax.ppermute(grad, 'pipe', swap)  7.99 us
    ppermute x5, starting transfers between devices, swap_sum(): other = lax.ppermute(x, axis, [(i, i ^ by) for i in range(peers)])  4.66 us
    pallas_call x1, Pallas kernels, shards(): pl.pallas_call(prep_kernel, out_shape=(jax.ShapeDtypeStruct((slots, width...  2.98 us
    ppermute x4, starting transfers between devices, shards(): below.append(lax.ppermute(grad, 'pipe', [(source, source - 1)]))  2.95 us
  transfers between devices with their start and end apart: 17, of which 6 were waited for; matrix products, arithmetic and copies ran while one was open for 3% of the time, Pallas kernels for 16%

profile of v1, /device:TPU:5, one launch (start us, length us, event | category | flops | bytes accessed | tf_op | source)
XLA Modules:
  0.0 98.0 jit_solution(16996509026635089981)
XLA Ops:
  0.7 1.2 %dynamic_slice.3 = s32[1]{0:T(128)} dynamic-slice(s32[4]{0:T(128)} %param.11, s32[]{:T(128)S(6)} %select_n.60), dynamic_slice_sizes={1} | dynamic-slice | bytes 12 | tf_op jit(solution)/shard_map/dynamic_slice | solution.py:200
  1.9 0.6 stack.38.place
  2.5 1.9 %copy-done = bf16[1,3,8,64,1024]{4,3,2,1,0:T(8,128)(2,1)S(1)} copy-done((bf16[1,3,8,64,1024]{4,3,2,1,0:T(8,128)(2,1)S(1)}, bf16[1,3,8,64,1024]{4,3,2,1,0:T(8,128)(2,1)}, u32[]{:S(2)}) %copy-start) | copy-done | bytes 3145752
  4.4 1.1 %copy-done.3 = bf16[1,3,8,128,128]{4,3,2,1,0:T(8,128)(2,1)S(1)} copy-done((bf16[1,3,8,128,128]{4,3,2,1,0:T(8,128)(2,1)S(1)}, bf16[1,3,8,128,128]{4,3,2,1,0:T(8,128)(2,1)}, u32[]{:S(2)}) %copy-start.3) | copy-done | bytes 786456
  5.6 1.2 %copy-done.7 = bf16[8,64,1024]{2,1,0:T(8,128)(2,1)S(1)} copy-done((bf16[8,64,1024]{2,1,0:T(8,128)(2,1)S(1)}, bf16[8,64,1024]{2,1,0:T(8,128)(2,1)}, u32[]{:S(2)}) %copy-start.7) | copy-done | bytes 1048600
  6.8 3.1 %chain.10 = (bf16[2,64,1024]{2,1,0:T(8,128)(2,1)S(1)}, bf16[3,2,64,1024]{3,2,1,0:T(8,128)(2,1)S(1)}) custom-call(s32[5]{0:T(128)S(1)} %stack.38.place, bf16[8,64,1024]{2,1,0:T(8,128)(2,1)S(1)} %copy-done.7, bf16[3,8,64,1024]{3,2,1,0:T(8,128)(2,1)S(1)} %bitcast.18, bf16[3,8,128,128]{3,2,1,0:T(8,128)(2,1)S(1)} %bitcast.26), custom_call_target="tpu_custom_call" | custom-call | tf_op jit(solution)/shard_map/chain/pallas_call | solution.py:232
  10.0 1.5 %collective-permute-done.refs_1_ = bf16[2,64,1024]{2,1,0:T(8,128)(2,1)S(1)} collective-permute-done((bf16[2,64,1024]{2,1,0:T(8,128)(2,1)S(1)}, bf16[2,64,1024]{2,1,0:T(8,128)(2,1)S(1)}, u32[]{:S(2)}, u32[]{:S(2)}) %collective-permute-start) | collective-permute-done | bytes 262176 | tf_op jit(solution)/shard_map/ppermute | solution.py:244
  11.5 5.2 %chain.11 = (bf16[2,64,1024]{2,1,0:T(8,128)(2,1)}, bf16[3,2,64,1024]{3,2,1,0:T(8,128)(2,1)S(1)}) custom-call(s32[5]{0:T(128)S(1)} %stack.38.place, bf16[8,64,1024]{2,1,0:T(8,128)(2,1)S(1)} %copy-done.7, bf16[2,64,1024]{2,1,0:T(8,128)(2,1)S(1)} %collective-permute-done.refs_1_, bf16[3,8,64,1024]{3,2,1,0:T(8,128)(2,1)} %bitcast.15, ...), custom_call_target="tpu_custom_call" | custom-call | tf_op jit(solution)/shard_map/chain/pallas_call | solution.py:232
  16.7 0.9 copy-done.12
  17.8 0.8 collective-permute-start.1
  18.6 0.9 collective-permute-done.2.refs_1_
  19.5 1.1 %copy-done.4 = bf16[1,3,8,128,128]{4,3,2,1,0:T(8,128)(2,1)S(1)} copy-done((bf16[1,3,8,128,128]{4,3,2,1,0:T(8,128)(2,1)S(1)}, bf16[1,3,8,128,128]{4,3,2,1,0:T(8,128)(2,1)}, u32[]{:S(2)}) %copy-start.4) | copy-done | bytes 786456
  20.6 1.2 %copy-done.8 = bf16[8,64,1024]{2,1,0:T(8,128)(2,1)S(1)} copy-done((bf16[8,64,1024]{2,1,0:T(8,128)(2,1)S(1)}, bf16[8,64,1024]{2,1,0:T(8,128)(2,1)}, u32[]{:S(2)}) %copy-start.8) | copy-done | bytes 1048600
  21.9 5.3 %chain.13 = (bf16[2,64,1024]{2,1,0:T(8,128)(2,1)}, bf16[3,2,64,1024]{3,2,1,0:T(8,128)(2,1)S(1)}) custom-call(s32[5]{0:T(128)S(1)} %stack.38.place, bf16[8,64,1024]{2,1,0:T(8,128)(2,1)S(1)} %copy-done.8, bf16[2,64,1024]{2,1,0:T(8,128)(2,1)} %collective-permute-done.2.refs_1_, bf16[3,8,64,1024]{3,2,1,0:T(8,128)(2,1)} %bitcast.16, ...), custom_call_target="tpu_custom_call" | custom-call | tf_op jit(solution)/shard_map/chain/pallas_call | solution.py:232
  27.1 0.9 copy-done.14
  28.0 0.1 collective-permute-start.5
  28.2 0.6 stack.35.place
  28.8 0.7 collective-permute-start.3
  29.5 1.1 %copy-done.5 = bf16[1,3,8,128,128]{4,3,2,1,0:T(8,128)(2,1)S(1)} copy-done((bf16[1,3,8,128,128]{4,3,2,1,0:T(8,128)(2,1)S(1)}, bf16[1,3,8,128,128]{4,3,2,1,0:T(8,128)(2,1)}, u32[]{:S(2)}) %copy-start.5) | copy-done | bytes 786456
  30.6 0.5 chain.12
  31.2 1.1 %collective-permute-start.4 = (bf16[2,64,1024]{2,1,0:T(8,128)(2,1)S(1)}, bf16[2,64,1024]{2,1,0:T(8,128)(2,1)S(1)}, u32[]{:S(2)}, u32[]{:S(2)}) collective-permute-start(bf16[2,64,1024]{2,1,0:T(8,128)(2,1)S(1)} %get-tuple-element.26), channel_id=1, source_target_pairs={{0,4},{4,0},{8,12},{12,8},{1,5},{5,1},{9,13},{13,9},{2,6},{6,2},{1... | collective-permute-start | bytes 786440 | tf_op jit(solution)/shard_map/ppermute | solution.py:244
  32.3 4.6 %chain.15 = (bf16[2,64,1024]{2,1,0:T(8,128)(2,1)S(1)}, bf16[3,2,64,1024]{3,2,1,0:T(8,128)(2,1)S(1)}) custom-call(s32[5]{0:T(128)S(1)} %stack.38.place, bf16[8,64,1024]{2,1,0:T(8,128)(2,1)S(1)} %copy-done.9, bf16[2,64,1024]{2,1,0:T(8,128)(2,1)} %collective-permute-done.5.refs_1_, bf16[3,8,64,1024]{3,2,1,0:T(8,128)(2,1)} %bitcast.17, ...), custom_call_target="tpu_custom_call" | custom-call | tf_op jit(solution)/shard_map/chain/pallas_call | solution.py:232
  36.9 0.8 collective-permute-start.6
  37.7 1.6 %collective-permute-start.8 = (bf16[2,64,1024]{2,1,0:T(8,128)(2,1)S(1)}, bf16[2,64,1024]{2,1,0:T(8,128)(2,1)S(1)}, u32[]{:S(2)}, u32[]{:S(2)}) collective-permute-start(bf16[2,64,1024]{2,1,0:T(8,128)(2,1)S(1)} %get-tuple-element.29), channel_id=1, source_target_pairs={{0,4},{4,0},{8,12},{12,8},{1,5},{5,1},{9,13},{13,9},{2,6},{6,2},{1... | collective-permute-start | bytes 786440 | tf_op jit(solution)/shard_map/ppermute | solution.py:244
  39.4 0.6 chain.14
  40.1 3.0 %prep.1 = (bf16[3,1024,128]{2,1,0:T(8,128)(2,1)S(1)}, bf16[3,256,128]{2,1,0:T(8,128)(2,1)S(1)}) custom-call(s32[5]{0:T(128)S(1)} %stack.38.place, s32[3,8]{1,0:T(4,128)S(1)} %bitcast.37, bf16[3,8,128,128]{3,2,1,0:T(8,128)(2,1)S(1)} %bitcast.36, bf16[3,8,64,1024]{3,2,1,0:T(8,128)(2,1)S(1)} %bitcast.21), custom_call_target="tpu_custom_call" | custom-call | tf_op jit(solution)/shard_map/prep/pallas_call | solution.py:208
  43.1 0.9 copy-done.16
  44.0 1.6 %collective-permute-start.12 = (bf16[3,256,128]{2,1,0:T(8,128)(2,1)S(1)}, bf16[3,256,128]{2,1,0:T(8,128)(2,1)S(1)}, u32[]{:S(2)}, u32[]{:S(2)}) collective-permute-start(bf16[3,256,128]{2,1,0:T(8,128)(2,1)S(1)} %get-tuple-element.45), channel_id=1, source_target_pairs={{0,1},{1,0},{2,3},{3,2},{4,5},{5,4},{6,7},{7,6},{8,9},{9,8},{10,11... | collective-permute-start | bytes 589832 | tf_op jit(solution)/shard_map/ppermute | solution.py:167
  45.5 0.6 chain.17
  46.1 0.7 collective-permute-start.9
  46.8 0.6 chain.16
  47.4 0.9 copy-done.17
  48.2 4.2 %collective-permute-start.10 = (bf16[2,64,1024]{2,1,0:T(8,128)(2,1)S(1)}, bf16[2,64,1024]{2,1,0:T(8,128)(2,1)S(1)}, u32[]{:S(2)}, u32[]{:S(2)}) collective-permute-start(bf16[2,64,1024]{2,1,0:T(8,128)(2,1)S(1)} %get-tuple-element.30), channel_id=1, source_target_pairs={{0,4},{4,0},{8,12},{12,8},{1,5},{5,1},{9,13},{13,9},{2,6},{6,2},{1... | collective-permute-start | bytes 786440 | tf_op jit(solution)/shard_map/ppermute | solution.py:244
  52.5 1.7 %collective-permute-start.13 = (bf16[3,256,128]{2,1,0:T(8,128)(2,1)S(1)}, bf16[3,256,128]{2,1,0:T(8,128)(2,1)S(1)}, u32[]{:S(2)}, u32[]{:S(2)}) collective-permute-start(bf16[3,256,128]{2,1,0:T(8,128)(2,1)S(1)} %add_convert_fusion.2), channel_id=1, source_target_pairs={{0,2},{1,3},{2,0},{3,1},{4,6},{5,7},{6,4},{7,5},{8,10},{9,11},{10,... | collective-permute-start | bytes 589832 | tf_op jit(solution)/shard_map/ppermute | solution.py:167
  54.2 0.6 chain.18
  54.8 0.9 copy-done.18
  55.7 0.6 collective-permute-start.11
  56.3 7.7 %collective-permute-done.13 = bf16[3,256,128]{2,1,0:T(8,128)(2,1)S(1)} collective-permute-done((bf16[3,256,128]{2,1,0:T(8,128)(2,1)S(1)}, bf16[3,256,128]{2,1,0:T(8,128)(2,1)S(1)}, u32[]{:S(2)}, u32[]{:S(2)}) %collective-permute-start.13) | collective-permute-done | bytes 196640 | tf_op jit(solution)/shard_map/ppermute | solution.py:167
  64.1 0.6 chain.19
  64.7 0.9 copy-done.19
  65.6 8.3 %sketch.1 = bf16[3,8,32,128]{3,2,1,0:T(8,128)(2,1)S(1)} custom-call(s32[5]{0:T(128)S(1)} %stack.38.place, bf16[3,2,64,1024]{3,2,1,0:T(8,128)(2,1)S(1)} %copy-done.11, bf16[3,2,64,1024]{3,2,1,0:T(8,128)(2,1)S(1)} %copy-done.13, bf16[3,2,64,1024]{3,2,1,0:T(8,128)(2,1)S(1)} %copy-done.15, bf16[3,2,64,1024]{3,2,1,0:T(8,128)(2,1)S(1)} %get-tuple-element.37.refs_3_, ...), custom_call_target="tpu_custom_call" | custom-call | tf_op jit(solution)/shard_map/sketch/pallas_call | solution.py:254
  73.9 1.3 %collective-permute-start.14 = (bf16[3,8,32,128]{3,2,1,0:T(8,128)(2,1)S(1)}, bf16[3,8,32,128]{3,2,1,0:T(8,128)(2,1)S(1)}, u32[]{:S(2)}, u32[]{:S(2)}) collective-permute-start(bf16[3,8,32,128]{3,2,1,0:T(8,128)(2,1)S(1)} %sketch.1), channel_id=1, source_target_pairs={{0,16},{16,0},{1,17},{17,1},{2,18},{18,2},{3,19},{19,3},{4,20},{20... | collective-permute-start | bytes 589832 | tf_op jit(solution)/shard_map/ppermute | solution.py:167
  75.2 4.8 %collective-permute-done.14 = bf16[3,8,32,128]{3,2,1,0:T(8,128)(2,1)S(1)} collective-permute-done((bf16[3,8,32,128]{3,2,1,0:T(8,128)(2,1)S(1)}, bf16[3,8,32,128]{3,2,1,0:T(8,128)(2,1)S(1)}, u32[]{:S(2)}, u32[]{:S(2)}) %collective-permute-start.14) | collective-permute-done | bytes 196640 | tf_op jit(solution)/shard_map/ppermute | solution.py:167
  80.1 5.1 %collective-permute-done.15 = bf16[3,8,32,128]{3,2,1,0:T(8,128)(2,1)S(1)} collective-permute-done((bf16[3,8,32,128]{3,2,1,0:T(8,128)(2,1)S(1)}, bf16[3,8,32,128]{3,2,1,0:T(8,128)(2,1)S(1)}, u32[]{:S(2)}, u32[]{:S(2)}) %collective-permute-start.15) | collective-permute-done | bytes 196640 | tf_op jit(solution)/shard_map/ppermute | solution.py:167
  85.4 1.2 %select_select_fusion.1 = (bf16[2,64,1024]{2,1,0:T(8,128)(2,1)S(1)}, bf16[2,64,1024]{2,1,0:T(8,128)(2,1)S(1)}, bf16[2,64,1024]{2,1,0:T(8,128)(2,1)S(1)}, bf16[2,64,1024]{2,1,0:T(8,128)(2,1)S(1)}) fusion(bf16[2,64,1024]{2,1,0:T(8,128)(2,1)S(1)} %copy-done.24, bf16[2,64,1024]{2,1,0:T(8,128)(2,1)S(1)} %copy-done.22, pred[]{:T(512)S(6)} %eq.9, pred[]{:T(512)S(6)} %eq.8, ...), kind=kLoop, calls=%fused_computation.7 | loop fusion | flops 1179648 | bytes 3670018 | tf_op jit(solution)/shard_map/jit(_where)/select_n | solution.py:270
  86.6 1.1 %maximum_bitcast_fusion = bf16[1,8,64,1024]{3,2,1,0:T(8,128)(2,1)} fusion(bf16[2,64,1024]{2,1,0:T(8,128)(2,1)S(1)} %get-tuple-element.49, bf16[2,64,1024]{2,1,0:T(8,128)(2,1)S(1)} %get-tuple-element.48, bf16[2,64,1024]{2,1,0:T(8,128)(2,1)S(1)} %get-tuple-element.47, bf16[2,64,1024]{2,1,0:T(8,128)(2,1)S(1)} %get-tuple-element.46), kind=kLoop, calls=%fused_computation | loop fusion | flops 1572864 | bytes 2097152 | tf_op jit(solution)/shard_map/broadcast_in_dim | solution.py:271
  87.7 9.4 %collective-permute-done.16 = bf16[3,8,32,128]{3,2,1,0:T(8,128)(2,1)S(1)} collective-permute-done((bf16[3,8,32,128]{3,2,1,0:T(8,128)(2,1)S(1)}, bf16[3,8,32,128]{3,2,1,0:T(8,128)(2,1)S(1)}, u32[]{:S(2)}, u32[]{:S(2)}) %collective-permute-start.16) | collective-permute-done | bytes 196640 | tf_op jit(solution)/shard_map/ppermute | solution.py:167
  97.2 0.8 broadcast_in_dim_reshape.3
  (62 shorter events, 0.8 us)
Async XLA Ops:
  2.5 1.9 %copy-start = (bf16[1,3,8,64,1024]{4,3,2,1,0:T(8,128)(2,1)S(1)}, bf16[1,3,8,64,1024]{4,3,2,1,0:T(8,128)(2,1)}, u32[]{:S(2)}) copy-start(bf16[1,3,8,64,1024]{4,3,2,1,0:T(8,128)(2,1)} %param.7) | copy-start | bytes 9437188
  4.4 1.1 %copy-start.3 = (bf16[1,3,8,128,128]{4,3,2,1,0:T(8,128)(2,1)S(1)}, bf16[1,3,8,128,128]{4,3,2,1,0:T(8,128)(2,1)}, u32[]{:S(2)}) copy-start(bf16[1,3,8,128,128]{4,3,2,1,0:T(8,128)(2,1)} %param.8) | copy-start | bytes 2359300
  5.6 1.2 %copy-start.7 = (bf16[8,64,1024]{2,1,0:T(8,128)(2,1)S(1)}, bf16[8,64,1024]{2,1,0:T(8,128)(2,1)}, u32[]{:S(2)}) copy-start(bf16[8,64,1024]{2,1,0:T(8,128)(2,1)} %refs_0_.7) | copy-start | bytes 3145732
  9.9 6.8 %copy-start.10 = (bf16[3,2,64,1024]{3,2,1,0:T(8,128)(2,1)}, bf16[3,2,64,1024]{3,2,1,0:T(8,128)(2,1)S(1)}, u32[]{:S(2)}) copy-start(bf16[3,2,64,1024]{3,2,1,0:T(8,128)(2,1)S(1)} %get-tuple-element.34.refs_0_) | copy-start | bytes 2359300
  9.9 7.7 %copy-start.21 = (bf16[2,64,1024]{2,1,0:T(8,128)(2,1)}, bf16[2,64,1024]{2,1,0:T(8,128)(2,1)S(1)}, u32[]{:S(2)}) copy-start(bf16[2,64,1024]{2,1,0:T(8,128)(2,1)S(1)} %get-tuple-element.24) | copy-start | bytes 786436
  9.9 1.6 %collective-permute-start = (bf16[2,64,1024]{2,1,0:T(8,128)(2,1)S(1)}, bf16[2,64,1024]{2,1,0:T(8,128)(2,1)S(1)}, u32[]{:S(2)}, u32[]{:S(2)}) collective-permute-start(bf16[2,64,1024]{2,1,0:T(8,128)(2,1)S(1)} %get-tuple-element.24), channel_id=1, source_target_pairs={{0,4},{4,0},{8,12},{12,8},{1,5},{5,1},{9,13},{13,9},{2,6},{6,2},{1... | collective-permute-start | bytes 786440 | tf_op jit(solution)/shard_map/ppermute | solution.py:244
  16.7 0.9 copy-start.12
  17.6 11.9 %copy-start.1 = (bf16[1,3,8,64,1024]{4,3,2,1,0:T(8,128)(2,1)S(1)}, bf16[1,3,8,64,1024]{4,3,2,1,0:T(8,128)(2,1)}, u32[]{:S(2)}) copy-start(bf16[1,3,8,64,1024]{4,3,2,1,0:T(8,128)(2,1)} %param.7) | copy-start | bytes 9437188
  17.6 1.9 %collective-permute-start.2 = (bf16[2,64,1024]{2,1,0:T(8,128)(2,1)}, bf16[2,64,1024]{2,1,0:T(8,128)(2,1)}, u32[]{:S(2)}, u32[]{:S(2)}) collective-permute-start(bf16[2,64,1024]{2,1,0:T(8,128)(2,1)} %get-tuple-element.25), channel_id=1, source_target_pairs={{0,4},{4,0},{8,12},{12,8},{1,5},{5,1},{9,13},{13,9},{2,6},{6,2},{1... | collective-permute-start | bytes 786440 | tf_op jit(solution)/shard_map/ppermute | solution.py:244
  17.8 11.7 %collective-permute-start.1 = (bf16[2,64,1024]{2,1,0:T(8,128)(2,1)}, bf16[2,64,1024]{2,1,0:T(8,128)(2,1)S(1)}, u32[]{:S(2)}, u32[]{:S(2)}) collective-permute-start(bf16[2,64,1024]{2,1,0:T(8,128)(2,1)} %get-tuple-element.25), channel_id=1, source_target_pairs={{8,4},{9,5},{10,6},{11,7},{24,20},{25,21},{26,22},{27,23}} | collective-permute-start | bytes 786440 | tf_op jit(solution)/shard_map/ppermute | solution.py:247
  19.5 1.1 %copy-start.4 = (bf16[1,3,8,128,128]{4,3,2,1,0:T(8,128)(2,1)S(1)}, bf16[1,3,8,128,128]{4,3,2,1,0:T(8,128)(2,1)}, u32[]{:S(2)}) copy-start(bf16[1,3,8,128,128]{4,3,2,1,0:T(8,128)(2,1)} %param.8) | copy-start | bytes 2359300
  20.6 1.2 %copy-start.8 = (bf16[8,64,1024]{2,1,0:T(8,128)(2,1)S(1)}, bf16[8,64,1024]{2,1,0:T(8,128)(2,1)}, u32[]{:S(2)}) copy-start(bf16[8,64,1024]{2,1,0:T(8,128)(2,1)} %refs_0_.7) | copy-start | bytes 3145732
  27.1 0.9 copy-start.14
  28.0 4.3 %collective-permute-start.5 = (bf16[2,64,1024]{2,1,0:T(8,128)(2,1)}, bf16[2,64,1024]{2,1,0:T(8,128)(2,1)}, u32[]{:S(2)}, u32[]{:S(2)}) collective-permute-start(bf16[2,64,1024]{2,1,0:T(8,128)(2,1)} %get-tuple-element.27), channel_id=1, source_target_pairs={{0,4},{4,0},{8,12},{12,8},{1,5},{5,1},{9,13},{13,9},{2,6},{6,2},{1... | collective-permute-start | bytes 786440 | tf_op jit(solution)/shard_map/ppermute | solution.py:244
  28.8 10.6 %collective-permute-start.3 = (bf16[2,64,1024]{2,1,0:T(8,128)(2,1)}, bf16[2,64,1024]{2,1,0:T(8,128)(2,1)S(1)}, u32[]{:S(2)}, u32[]{:S(2)}) collective-permute-start(bf16[2,64,1024]{2,1,0:T(8,128)(2,1)} %get-tuple-element.27), channel_id=1, source_target_pairs={{8,4},{9,5},{10,6},{11,7},{24,20},{25,21},{26,22},{27,23}} | collective-permute-start | bytes 786440 | tf_op jit(solution)/shard_map/ppermute | solution.py:247
  29.5 1.1 %copy-start.5 = (bf16[1,3,8,128,128]{4,3,2,1,0:T(8,128)(2,1)S(1)}, bf16[1,3,8,128,128]{4,3,2,1,0:T(8,128)(2,1)}, u32[]{:S(2)}) copy-start(bf16[1,3,8,128,128]{4,3,2,1,0:T(8,128)(2,1)} %param.8) | copy-start | bytes 2359300
  30.6 1.7 %copy-start.6 = (bf16[1,3,8,128,128]{4,3,2,1,0:T(8,128)(2,1)S(1)}, bf16[1,3,8,128,128]{4,3,2,1,0:T(8,128)(2,1)}, u32[]{:S(2)}) copy-start(bf16[1,3,8,128,128]{4,3,2,1,0:T(8,128)(2,1)} %param.8) | copy-start | bytes 2359300
  30.6 1.7 %copy-start.9 = (bf16[8,64,1024]{2,1,0:T(8,128)(2,1)S(1)}, bf16[8,64,1024]{2,1,0:T(8,128)(2,1)}, u32[]{:S(2)}) copy-start(bf16[8,64,1024]{2,1,0:T(8,128)(2,1)} %refs_0_.7) | copy-start | bytes 3145732
  31.2 8.7 %copy-start.23 = (bf16[2,64,1024]{2,1,0:T(8,128)(2,1)}, bf16[2,64,1024]{2,1,0:T(8,128)(2,1)S(1)}, u32[]{:S(2)}) copy-start(bf16[2,64,1024]{2,1,0:T(8,128)(2,1)S(1)} %get-tuple-element.26) | copy-start | bytes 786436
  31.2 8.2 %copy-start.2 = (bf16[1,3,8,64,1024]{4,3,2,1,0:T(8,128)(2,1)S(1)}, bf16[1,3,8,64,1024]{4,3,2,1,0:T(8,128)(2,1)}, u32[]{:S(2)}) copy-start(bf16[1,3,8,64,1024]{4,3,2,1,0:T(8,128)(2,1)} %param.7) | copy-start | bytes 9437188
  31.2 8.1 %collective-permute-start.4 = (bf16[2,64,1024]{2,1,0:T(8,128)(2,1)S(1)}, bf16[2,64,1024]{2,1,0:T(8,128)(2,1)S(1)}, u32[]{:S(2)}, u32[]{:S(2)}) collective-permute-start(bf16[2,64,1024]{2,1,0:T(8,128)(2,1)S(1)} %get-tuple-element.26), channel_id=1, source_target_pairs={{0,4},{4,0},{8,12},{12,8},{1,5},{5,1},{9,13},{13,9},{2,6},{6,2},{1... | collective-permute-start | bytes 786440 | tf_op jit(solution)/shard_map/ppermute | solution.py:244
  36.9 3.2 %copy-start.25 = (s32[1,3,8]{2,0,1:T(1,128)S(1)}, s32[1,3,8]{2,0,1:T(1,128)}, u32[]{:S(2)}) copy-start(s32[1,3,8]{2,0,1:T(1,128)} %param.10) | copy-start | bytes 292
  36.9 3.1 %copy-start.20 = (bf16[1,3,8,128,128]{4,3,2,1,0:T(8,128)(2,1)S(1)}, bf16[1,3,8,128,128]{4,3,2,1,0:T(8,128)(2,1)}, u32[]{:S(2)}) copy-start(bf16[1,3,8,128,128]{4,3,2,1,0:T(8,128)(2,1)} %param.9) | copy-start | bytes 2359300
  36.9 9.8 %collective-permute-start.6 = (bf16[2,64,1024]{2,1,0:T(8,128)(2,1)S(1)}, bf16[2,64,1024]{2,1,0:T(8,128)(2,1)S(1)}, u32[]{:S(2)}, u32[]{:S(2)}) collective-permute-start(bf16[2,64,1024]{2,1,0:T(8,128)(2,1)S(1)} %get-tuple-element.29), channel_id=1, source_target_pairs={{8,4},{9,5},{10,6},{11,7},{24,20},{25,21},{26,22},{27,23}} | collective-permute-start | bytes 786440 | tf_op jit(solution)/shard_map/ppermute | solution.py:247
  37.7 7.8 %collective-permute-start.8 = (bf16[2,64,1024]{2,1,0:T(8,128)(2,1)S(1)}, bf16[2,64,1024]{2,1,0:T(8,128)(2,1)S(1)}, u32[]{:S(2)}, u32[]{:S(2)}) collective-permute-start(bf16[2,64,1024]{2,1,0:T(8,128)(2,1)S(1)} %get-tuple-element.29), channel_id=1, source_target_pairs={{0,4},{4,0},{8,12},{12,8},{1,5},{5,1},{9,13},{13,9},{2,6},{6,2},{1... | collective-permute-start | bytes 786440 | tf_op jit(solution)/shard_map/ppermute | solution.py:244
  40.0 6.8 %collective-permute-start.7 = (bf16[2,64,1024]{2,1,0:T(8,128)(2,1)S(1)}, bf16[2,64,1024]{2,1,0:T(8,128)(2,1)S(1)}, u32[]{:S(2)}, u32[]{:S(2)}) collective-permute-start(bf16[2,64,1024]{2,1,0:T(8,128)(2,1)S(1)} %get-tuple-element.28), channel_id=1, source_target_pairs={{0,4},{4,0},{8,12},{12,8},{1,5},{5,1},{9,13},{13,9},{2,6},{6,2},{1... | collective-permute-start | bytes 786440 | tf_op jit(solution)/shard_map/ppermute | solution.py:244
  43.0 0.9 copy-start.16
  44.0 8.5 %collective-permute-start.12 = (bf16[3,256,128]{2,1,0:T(8,128)(2,1)S(1)}, bf16[3,256,128]{2,1,0:T(8,128)(2,1)S(1)}, u32[]{:S(2)}, u32[]{:S(2)}) collective-permute-start(bf16[3,256,128]{2,1,0:T(8,128)(2,1)S(1)} %get-tuple-element.45), channel_id=1, source_target_pairs={{0,1},{1,0},{2,3},{3,2},{4,5},{5,4},{6,7},{7,6},{8,9},{9,8},{10,11... | collective-permute-start | bytes 589832 | tf_op jit(solution)/shard_map/ppermute | solution.py:167
  46.1 8.2 %collective-permute-start.9 = (bf16[2,64,1024]{2,1,0:T(8,128)(2,1)S(1)}, bf16[2,64,1024]{2,1,0:T(8,128)(2,1)S(1)}, u32[]{:S(2)}, u32[]{:S(2)}) collective-permute-start(bf16[2,64,1024]{2,1,0:T(8,128)(2,1)S(1)} %get-tuple-element.31), channel_id=1, source_target_pairs={{8,4},{9,5},{10,6},{11,7},{24,20},{25,21},{26,22},{27,23}} | collective-permute-start | bytes 786440 | tf_op jit(solution)/shard_map/ppermute | solution.py:247
  47.4 0.9 copy-start.17
  48.2 6.0 %collective-permute-start.10 = (bf16[2,64,1024]{2,1,0:T(8,128)(2,1)S(1)}, bf16[2,64,1024]{2,1,0:T(8,128)(2,1)S(1)}, u32[]{:S(2)}, u32[]{:S(2)}) collective-permute-start(bf16[2,64,1024]{2,1,0:T(8,128)(2,1)S(1)} %get-tuple-element.30), channel_id=1, source_target_pairs={{0,4},{4,0},{8,12},{12,8},{1,5},{5,1},{9,13},{13,9},{2,6},{6,2},{1... | collective-permute-start | bytes 786440 | tf_op jit(solution)/shard_map/ppermute | solution.py:244
  52.5 11.5 %collective-permute-start.13 = (bf16[3,256,128]{2,1,0:T(8,128)(2,1)S(1)}, bf16[3,256,128]{2,1,0:T(8,128)(2,1)S(1)}, u32[]{:S(2)}, u32[]{:S(2)}) collective-permute-start(bf16[3,256,128]{2,1,0:T(8,128)(2,1)S(1)} %add_convert_fusion.2), channel_id=1, source_target_pairs={{0,2},{1,3},{2,0},{3,1},{4,6},{5,7},{6,4},{7,5},{8,10},{9,11},{10,... | collective-permute-start | bytes 589832 | tf_op jit(solution)/shard_map/ppermute | solution.py:167
  54.8 0.9 copy-start.18
  55.7 9.9 %copy-start.11 = (bf16[3,2,64,1024]{3,2,1,0:T(8,128)(2,1)S(1)}, bf16[3,2,64,1024]{3,2,1,0:T(8,128)(2,1)}, u32[]{:S(2)}) copy-start(bf16[3,2,64,1024]{3,2,1,0:T(8,128)(2,1)} %copy-done.10) | copy-start | bytes 2359300
  55.7 9.9 %copy-start.13 = (bf16[3,2,64,1024]{3,2,1,0:T(8,128)(2,1)S(1)}, bf16[3,2,64,1024]{3,2,1,0:T(8,128)(2,1)}, u32[]{:S(2)}) copy-start(bf16[3,2,64,1024]{3,2,1,0:T(8,128)(2,1)} %copy-done.12) | copy-start | bytes 2359300
  55.7 9.9 %copy-start.15 = (bf16[3,2,64,1024]{3,2,1,0:T(8,128)(2,1)S(1)}, bf16[3,2,64,1024]{3,2,1,0:T(8,128)(2,1)}, u32[]{:S(2)}) copy-start(bf16[3,2,64,1024]{3,2,1,0:T(8,128)(2,1)} %copy-done.14) | copy-start | bytes 2359300
  55.7 8.4 %collective-permute-start.11 = (bf16[2,64,1024]{2,1,0:T(8,128)(2,1)S(1)}, bf16[2,64,1024]{2,1,0:T(8,128)(2,1)S(1)}, u32[]{:S(2)}, u32[]{:S(2)}) collective-permute-start(bf16[2,64,1024]{2,1,0:T(8,128)(2,1)S(1)} %get-tuple-element.32), channel_id=1, source_target_pairs={{0,4},{4,0},{8,12},{12,8},{1,5},{5,1},{9,13},{13,9},{2,6},{6,2},{1... | collective-permute-start | bytes 786440 | tf_op jit(solution)/shard_map/ppermute | solution.py:244
  64.7 0.9 copy-start.19
  65.6 19.8 %copy-start.22 = (bf16[2,64,1024]{2,1,0:T(8,128)(2,1)S(1)}, bf16[2,64,1024]{2,1,0:T(8,128)(2,1)}, u32[]{:S(2)}) copy-start(bf16[2,64,1024]{2,1,0:T(8,128)(2,1)} %copy-done.21) | copy-start | bytes 786436
  65.6 19.8 %copy-start.24 = (bf16[2,64,1024]{2,1,0:T(8,128)(2,1)S(1)}, bf16[2,64,1024]{2,1,0:T(8,128)(2,1)}, u32[]{:S(2)}) copy-start(bf16[2,64,1024]{2,1,0:T(8,128)(2,1)} %copy-done.23) | copy-start | bytes 786436
  73.9 6.1 %collective-permute-start.14 = (bf16[3,8,32,128]{3,2,1,0:T(8,128)(2,1)S(1)}, bf16[3,8,32,128]{3,2,1,0:T(8,128)(2,1)S(1)}, u32[]{:S(2)}, u32[]{:S(2)}) collective-permute-start(bf16[3,8,32,128]{3,2,1,0:T(8,128)(2,1)S(1)} %sketch.1), channel_id=1, source_target_pairs={{0,16},{16,0},{1,17},{17,1},{2,18},{18,2},{3,19},{19,3},{4,20},{20... | collective-permute-start | bytes 589832 | tf_op jit(solution)/shard_map/ppermute | solution.py:167
  80.0 5.2 %collective-permute-start.15 = (bf16[3,8,32,128]{3,2,1,0:T(8,128)(2,1)S(1)}, bf16[3,8,32,128]{3,2,1,0:T(8,128)(2,1)S(1)}, u32[]{:S(2)}, u32[]{:S(2)}) collective-permute-start(bf16[3,8,32,128]{3,2,1,0:T(8,128)(2,1)S(1)} %add_convert_fusion.1), channel_id=1, source_target_pairs={{0,1},{1,0},{2,3},{3,2},{4,5},{5,4},{6,7},{7,6},{8,9},{9,8},{10,11... | collective-permute-start | bytes 589832 | tf_op jit(solution)/shard_map/ppermute | solution.py:167
  85.3 11.8 %collective-permute-start.16 = (bf16[3,8,32,128]{3,2,1,0:T(8,128)(2,1)S(1)}, bf16[3,8,32,128]{3,2,1,0:T(8,128)(2,1)S(1)}, u32[]{:S(2)}, u32[]{:S(2)}) collective-permute-start(bf16[3,8,32,128]{3,2,1,0:T(8,128)(2,1)S(1)} %add_convert_fusion), channel_id=1, source_target_pairs={{0,2},{1,3},{2,0},{3,1},{4,6},{5,7},{6,4},{7,5},{8,10},{9,11},{10,... | collective-permute-start | bytes 589832 | tf_op jit(solution)/shard_map/ppermute | solution.py:167

commit v2 on v1

v2 whole, which is shorter than its diff:
```python
import functools
import math

import jax
import jax.numpy as jnp
from jax import lax
from jax.experimental import pallas as pl
from jax.experimental.pallas import tpu as pltpu
from jax.sharding import PartitionSpec as P

F32 = jnp.float32
BF16 = jnp.bfloat16
VMEM = pl.BlockSpec(memory_space=pltpu.VMEM)
SMEM = pl.BlockSpec(memory_space=pltpu.SMEM)
ANY = pl.BlockSpec(memory_space=pl.ANY)
PARAMS = pltpu.CompilerParams(vmem_limit_bytes=16 * 1024 * 1024)
NN = (((1,), (0,)), ((), ()))
NT = (((1,), (1,)), ((), ()))


def mm(a, b, dims=NN):
    return lax.dot_general(a, b, dims, preferred_element_type=F32)


def silu_slope(value):
    sig = 0.5 + 0.5 * jnp.tanh(0.5 * value)
    return sig * (1.0 + value * (1.0 - sig))


def left_lanes(shape, rank):
    return lax.broadcasted_iota(jnp.int32, shape, len(shape) - 1) < rank


def head_lanes(h, head_size):
    return slice(h * head_size, (h + 1) * head_size)


def slopes_of(k, at, acts, mixing, slopes):
    chunk, tokens, width = slopes.shape[1:]
    heads, head_size = mixing.shape[1], mixing.shape[2]
    pre = []
    for h in range(heads):
        act = acts[k, at : at + chunk, :, head_lanes(h, head_size)].reshape(chunk * tokens, head_size)
        pre.append(mm(act, mixing[k, h]))
    for h in range(heads):
        slopes[k, :, :, head_lanes(h, head_size)] = silu_slope(pre[h]).reshape(chunk, tokens, head_size)


def chain(live, source, slopes, mixing, grad, deltas):
    chunk, tokens, width = grad.shape
    heads, head_size = mixing.shape[1], mixing.shape[2]
    rows = chunk * tokens
    grad[...] = source

    def slot(i, _):
        k = live - 1 - i
        old, delta = [], []
        for h in range(heads):
            lanes = head_lanes(h, head_size)
            g = grad[:, :, lanes].reshape(rows, head_size).astype(F32)
            old.append(g)
            delta.append((g * slopes[k, :, :, lanes].reshape(rows, head_size)).astype(BF16))
        back = [mm(delta[h], mixing[k, h], NT) for h in range(heads)]
        for h in range(heads):
            lanes = head_lanes(h, head_size)
            deltas[k, :, :, lanes] = delta[h].reshape(chunk, tokens, head_size)
            grad[:, :, lanes] = (old[h] + back[h]).astype(BF16).reshape(chunk, tokens, head_size)
        return 0

    lax.fori_loop(0, live, slot, 0)


def here(pair):
    section = lax.axis_index("pipe")
    return section // 2 == pair, section % 2 == 1


def first_kernel(pair, sizes, top, acts, mixing, grad, deltas, slopes, acts_v, mixing_v, top_v, sems):
    slots = acts.shape[0]
    chunk, micro = grad.shape[0], acts.shape[1]
    section = lax.axis_index("pipe")
    live = sizes[section]
    copies = []

    def load(src, dst):
        copy = pltpu.make_async_copy(src, dst, sems.at[len(copies)])
        copy.start()
        copies.append(copy)
        return copy

    need = {}
    for k in range(slots - 1, -1, -1):
        need[k] = (
            load(mixing.at[k], mixing_v.at[k]),
            load(acts.at[k, pl.ds(0, chunk)], acts_v.at[k, pl.ds(0, chunk)]),
        )
    first = load(top.at[pl.ds(0, chunk)], top_v.at[pl.ds(0, chunk)])
    rest = [load(acts.at[k, pl.ds(chunk, micro - chunk)], acts_v.at[k, pl.ds(chunk, micro - chunk)]) for k in range(slots)]
    rest.append(load(top.at[pl.ds(chunk, micro - chunk)], top_v.at[pl.ds(chunk, micro - chunk)]))
    for k in range(slots - 1, -1, -1):
        for copy in need[k]:
            copy.wait()

        @pl.when(k < live)
        def _():
            slopes_of(k, 0, acts_v, mixing_v, slopes)

    first.wait()
    active, odd = here(pair)

    @pl.when(jnp.logical_and(active, odd))
    def _():
        chain(live, top_v[:chunk], slopes, mixing_v, grad, deltas)

    for copy in rest:
        copy.wait()


def slope_kernel(at, sizes, acts, mixing, slopes):
    section = lax.axis_index("pipe")
    live = sizes[section]

    for k in range(acts.shape[0]):

        @pl.when(k < live)
        def _():
            slopes_of(k, at, acts, mixing, slopes)


def chain_kernel(pair, odd_at, has_odd, has_even, sizes, mixing, *refs):
    refs = list(refs)
    odd_in, odd_slopes = (refs.pop(0), refs.pop(0)) if has_odd else (None, None)
    even_in, even_slopes = (refs.pop(0), refs.pop(0)) if has_even else (None, None)
    grad, deltas = refs
    chunk = grad.shape[0]
    section = lax.axis_index("pipe")
    live = sizes[section]
    active, odd = here(pair)

    if has_odd:

        @pl.when(jnp.logical_and(active, odd))
        def _():
            chain(live, odd_in[odd_at : odd_at + chunk], odd_slopes, mixing, grad, deltas)

    if has_even:

        @pl.when(jnp.logical_and(active, jnp.logical_not(odd)))
        def _():
            chain(live, even_in[...], even_slopes, mixing, grad, deltas)


def prep_kernel(blocks, tiles, acts, dense_g, act_sums, dense_a):
    slots, picks, head_size, both = tiles.shape
    rank = both // 2
    micro = acts.shape[1]
    heads = dense_a.shape[1] // head_size
    first_head = lax.axis_index("tensor") * heads
    row = lax.broadcasted_iota(jnp.int32, (both, both), 0)
    col = lax.broadcasted_iota(jnp.int32, (both, both), 1)
    twice = (row == col % rank).astype(BF16)
    row = lax.broadcasted_iota(jnp.int32, (rank, both), 0)
    col = lax.broadcasted_iota(jnp.int32, (rank, both), 1)
    split = (col == rank + jnp.where(row < rank // 2, 2 * row, 2 * row - rank + 1)).astype(BF16)
    dense_a[...] = jnp.zeros_like(dense_a)
    dense_g[...] = jnp.zeros_like(dense_g)
    for k in range(slots):
        for j in range(picks):
            own = blocks[k, j] - first_head

            @pl.when(jnp.logical_and(own >= 0, own < heads))
            def _():
                place = pl.ds(pl.multiple_of(own * head_size, head_size), head_size)
                tile = tiles[k, j]
                dense_a[k, place, :] = mm(tile, twice).astype(BF16)
                dense_g[k, :, place] = mm(split, tile, NT).astype(BF16)

    half = micro // 2
    tokens = acts.shape[2]

    def project(k, _):
        one = mm(acts[k, :half].reshape(half * tokens, -1), dense_a[k])
        two = mm(acts[k, half:].reshape(half * tokens, -1), dense_a[k])
        act_sums[k] = jnp.where(left_lanes(one.shape, rank), one, two).astype(BF16)
        return 0

    lax.fori_loop(0, slots, project, 0)


def sketch_kernel(chunks, pairs, scale, sizes, *refs):
    per = len(chunks) + 1
    deltas = [refs[p * per : (p + 1) * per] for p in range(pairs)]
    dense_g, act_sums, out = refs[pairs * per :]
    slots, chunk, tokens, width = deltas[0][0].shape
    rank = dense_g.shape[1]
    both = 2 * rank
    rows = chunk * tokens
    half = act_sums.shape[1]
    section = lax.axis_index("pipe")
    live = sizes[section]

    def one(ref, i):
        start = chunks[i] * rows
        token = lax.broadcasted_iota(jnp.int32, (rows, both), 0) // tokens
        for k in range(slots):

            @pl.when(k < live)
            def _():
                proj = mm(dense_g[k], ref[k].reshape(rows, width), NT).astype(BF16)
                act = act_sums[k, start % half : start % half + rows]
                other = pltpu.roll(act, rank, 1)
                left = left_lanes(act.shape, rank)
                act = jnp.where(left, act, other) if start < half else jnp.where(left, other, act)
                spread = jnp.concatenate([jnp.where(token == m, act, 0.0) for m in range(chunk)], axis=1)
                full = mm(proj, spread.astype(BF16))
                for m in range(chunk):
                    even = full[: rank // 2, m * both : (m + 1) * both]
                    uneven = full[rank // 2 :, m * both : (m + 1) * both]
                    res = jnp.where(left_lanes(even.shape, rank), even, uneven) * scale
                    out[k, i * chunk + m] = res.astype(BF16)

            @pl.when(k >= live)
            def _():
                out[k, i * chunk : (i + 1) * chunk] = jnp.zeros((chunk, rank // 2, both), BF16)

    for i in range(len(chunks)):
        for p in range(pairs):
            active, odd = here(pairs - 1 - p)

            @pl.when(jnp.logical_and(active, odd))
            def _():
                one(deltas[p][i], i)

            @pl.when(jnp.logical_and(active, jnp.logical_not(odd)))
            def _():
                one(deltas[p][i + 1], i)


def swap_sum(x, axis, by):
    peers = lax.axis_size(axis)
    other = lax.ppermute(x, axis, [(i, i ^ by) for i in range(peers)])
    return x.astype(F32) + other.astype(F32)


def all_sum(x, axes):
    x = x.astype(BF16)
    total = x.astype(F32)
    for axis in axes:
        peers = lax.axis_size(axis)
        if peers & (peers - 1):
            total = lax.psum(total, axis)
        else:
            by = 1
            while by < peers:
                total = swap_sum(total.astype(BF16), axis, by)
                by *= 2
    return total


def shards(grad_out, activations, mixing, proj_tiles, proj_blocks, section_sizes):
    sections = lax.axis_size("pipe")
    section = lax.axis_index("pipe")
    micro, tokens, width = grad_out.shape
    slots = activations.shape[1]
    rank = proj_tiles.shape[4] // 2
    scale = 1.0 / math.sqrt(tokens * lax.axis_size("dp"))
    pairs = sections // 2
    count = 4
    chunk = micro // count
    pair = section // 2

    def call(kernel, name, ins, specs, outs, scratch=()):
        outs = tuple(jax.ShapeDtypeStruct(s, t) for s, t in outs)
        return pl.pallas_call(
            kernel,
            out_shape=outs,
            in_specs=specs,
            out_specs=(VMEM,) * len(outs),
            scratch_shapes=scratch,
            compiler_params=PARAMS,
            name=name,
        )(*ins)

    step_outs = [((chunk, tokens, width), BF16), ((slots, chunk, tokens, width), BF16)]
    slope_out = ((slots, chunk, tokens, width), F32)
    grad, delta, slope, acts, mix, top = call(
        functools.partial(first_kernel, pairs - 1),
        "first",
        (section_sizes, grad_out, activations[0], mixing[0]),
        [SMEM, ANY, ANY, ANY],
        step_outs
        + [slope_out, (activations.shape[1:], BF16), (mixing.shape[1:], BF16), (grad_out.shape, BF16)],
        [pltpu.SemaphoreType.DMA((3 * slots + 2,))],
    )
    slopes = [slope]

    swap = [(i, i ^ 1) for i in range(sections)]
    from_above = [(top, c * chunk) for c in range(count)]
    all_deltas, all_grads = [], []
    for p in range(pairs):
        deltas, grads, below = [], [], []
        even_in = None
        for step in range(count + 1):
            if p > 0 or step > 0:
                ins, specs = [section_sizes, mix], [SMEM, VMEM]
                has_odd, has_even = step < count, step > 0
                odd_at = 0
                if has_odd:
                    source, odd_at = from_above[step]
                    ins += [source, slopes[step]]
                if has_even:
                    ins += [even_in, slopes[step - 1]]
                specs += [VMEM] * (len(ins) - 2)
                kernel = functools.partial(chain_kernel, pairs - 1 - p, odd_at, has_odd, has_even)
                grad, delta = call(kernel, "chain", ins, specs, step_outs)
            if step < count:
                even_in = lax.ppermute(grad, "pipe", swap)
            if step > 0 and p + 1 < pairs:
                source = sections - 2 - 2 * p
                below.append((lax.ppermute(grad, "pipe", [(source, source - 1)]), 0))
            grads.append(grad)
            deltas.append(delta)
            if p == 0 and step + 1 < count:
                slopes += call(
                    functools.partial(slope_kernel, (step + 1) * chunk),
                    "slope",
                    (section_sizes, acts, mix),
                    [SMEM, VMEM, VMEM],
                    [slope_out],
                )
        from_above = below
        all_deltas.append(deltas)
        all_grads.append(grads)

    dense_g, act_part = call(
        prep_kernel,
        "prep",
        (proj_blocks[0], proj_tiles[0], acts),
        [SMEM, VMEM, VMEM],
        [((slots, rank, width), BF16), ((slots, micro // 2 * tokens, 2 * rank), BF16)],
        [pltpu.VMEM((slots, width, 2 * rank), BF16)],
    )
    act_sums = all_sum(act_part, ("tensor",))

    parts = []
    for chunks in (range(0, count // 2), range(count // 2, count)):
        ins = [section_sizes]
        for deltas in all_deltas:
            ins += deltas[chunks[0] : chunks[-1] + 2]
        ins += [dense_g, act_sums]
        (part,) = call(
            functools.partial(sketch_kernel, list(chunks), pairs, scale),
            "sketch",
            ins,
            [SMEM] + [VMEM] * (len(ins) - 1),
            [((slots, len(chunks) * chunk, rank // 2, 2 * rank), BF16)],
        )
        parts.append(all_sum(part, ("dp", "tensor")))
    sketch = jnp.concatenate(parts, axis=1).reshape(slots, micro, rank * rank)

    picked = []
    for step in range(count + 1):
        value = all_grads[0][step]
        for p in range(1, pairs):
            value = jnp.where(pair == pairs - 1 - p, all_grads[p][step], value)
        picked.append(value)
    segment_out = jnp.concatenate([jnp.where(section % 2 == 1, picked[c], picked[c + 1]) for c in range(count)])
    return (segment_out[None], sketch[None])


def solution(mesh):
    return jax.shard_map(
        shards,
        mesh=mesh,
        in_specs=(
            P(None, "dp", "tensor"),
            P("pipe", None, None, "dp", "tensor"),
            P("pipe", None, "tensor", None, None),
            P("pipe", None, None, None, None),
            P("pipe", None, None),
            P(),
        ),
        out_specs=(P("pipe", None, "dp", "tensor"), P("pipe", None, None, None)),
        check_vma=False,
    )
```

time: 98.1 us -> 78.7 us (0.80)
  the two profiles are of different devices: /device:TPU:5 before, /device:TPU:0 now
where the time goes in v2:
time: 78.7 us; the launch traced here: 80.2 us
  Pallas kernels  24.7 us (31%)
  starting transfers between devices  22.9 us (29%)
  waiting for transfers between devices  18.2 us (23%)
  local copies, waits for them, and re-layouts  8.98 us (11%)
  other arithmetic  4.09 us (5%)
  between operations  1.25 us (2%)
    pallas_call x16, Pallas kernels, call(): pl.pallas_call(kernel, out_shape=outs, in_specs=specs, out_specs=(VMEM,)...  24.7 us
    ppermute x8, waiting for transfers between devices, swap_sum(): other = lax.ppermute(x, axis, [(i, i ^ by) for i in range(peers)])  17.4 us
    ppermute x8, starting transfers between devices, swap_sum(): other = lax.ppermute(x, axis, [(i, i ^ by) for i in range(peers)])  13.6 us
    unnamed x67, local copies, waits for them, and re-layouts  8.16 us
    ppermute x8, starting transfers between devices, shards(): even_in = lax.ppermute(grad, 'pipe', swap)  6.6 us
    ppermute x4, starting transfers between devices, shards(): below.append((lax.ppermute(grad, 'pipe', [(source, source - 1)]), 0))  2.69 us
  transfers between devices with their start and end apart: 20, of which 7 were waited for; matrix products, arithmetic and copies ran while one was open for 5% of the time, Pallas kernels for 28%

profile of v2, /device:TPU:0, one launch (start us, length us, event | category | flops | bytes accessed | tf_op | source)
XLA Modules:
  0.0 80.2 jit_solution(13896563458499855669)
XLA Ops:
  0.6 1.9 %copy-done = bf16[1,3,8,64,1024]{4,3,2,1,0:T(8,128)(2,1)S(1)} copy-done((bf16[1,3,8,64,1024]{4,3,2,1,0:T(8,128)(2,1)S(1)}, bf16[1,3,8,64,1024]{4,3,2,1,0:T(8,128)(2,1)}, u32[]{:S(2)}) %copy-start) | copy-done | bytes 3145752
  2.5 1.2 %copy-done.5 = bf16[8,64,1024]{2,1,0:T(8,128)(2,1)S(1)} copy-done((bf16[8,64,1024]{2,1,0:T(8,128)(2,1)S(1)}, bf16[8,64,1024]{2,1,0:T(8,128)(2,1)}, u32[]{:S(2)}) %copy-start.5) | copy-done | bytes 1048600
  3.7 1.1 %copy-done.6 = bf16[1,3,8,128,128]{4,3,2,1,0:T(8,128)(2,1)S(1)} copy-done((bf16[1,3,8,128,128]{4,3,2,1,0:T(8,128)(2,1)S(1)}, bf16[1,3,8,128,128]{4,3,2,1,0:T(8,128)(2,1)}, u32[]{:S(2)}) %copy-start.6) | copy-done | bytes 786456
  4.9 0.7 copy-done.30
  5.5 2.0 %first.1 = (bf16[2,64,1024]{2,1,0:T(8,128)(2,1)S(1)}, bf16[3,2,64,1024]{3,2,1,0:T(8,128)(2,1)S(1)}, f32[3,2,64,1024]{3,2,1,0:T(8,128)S(1)}, bf16[3,8,64,1024]{3,...) custom-call(s32[4]{0:T(128)S(1)} %copy-done.30, ...), custom_call_target="tpu_custom_call" | custom-call | tf_op jit(solution)/shard_map/first/pallas_call | solution.py:274
  7.6 1.5 %slope.3.refs_1_.refs_3_ = f32[3,2,64,1024]{3,2,1,0:T(8,128)S(1)} custom-call(s32[4]{0:T(128)S(1)} %copy-done.30, bf16[3,8,64,1024]{3,2,1,0:T(8,128)(2,1)S(1)} %get-tuple-element.30.acts, bf16[3,8,128,128]{3,2,1,0:T(8,128)(2,1)S(1)} %get-tuple-element.28.mixing), custom_call_target="tpu_custom_call" | custom-call | tf_op jit(solution)/shard_map/slope/pallas_call | solution.py:274
  9.1 0.6 chain.9
  9.9 0.7 collective-permute-start.1
  10.6 2.9 %prep.1 = (bf16[3,64,1024]{2,1,0:T(8,128)(2,1)S(1)}, bf16[3,256,128]{2,1,0:T(8,128)(2,1)S(1)}) custom-call(s32[3,8]{1,0:T(4,128)S(1)} %bitcast.13, bf16[3,8,128,128]{3,2,1,0:T(8,128)(2,1)S(1)} %bitcast.12, bf16[3,8,64,1024]{3,2,1,0:T(8,128)(2,1)S(1)} %get-tuple-element.30.acts), custom_call_target="tpu_custom_call" | custom-call | tf_op jit(solution)/shard_map/prep/pallas_call | solution.py:274
  13.6 2.9 %collective-permute-start.12 = (bf16[3,256,128]{2,1,0:T(8,128)(2,1)S(1)}, bf16[3,256,128]{2,1,0:T(8,128)(2,1)S(1)}, u32[]{:S(2)}, u32[]{:S(2)}) collective-permute-start(bf16[3,256,128]{2,1,0:T(8,128)(2,1)S(1)} %get-tuple-element.49), channel_id=1, source_target_pairs={{0,1},{1,0},{2,3},{3,2},{4,5},{5,4},{6,7},{7,6},{8,9},{9,8},{10,11... | collective-permute-start | bytes 589832 | tf_op jit(solution)/shard_map/ppermute | solution.py:241
  16.5 1.5 %slope.4.refs_1_.refs_3_ = f32[3,2,64,1024]{3,2,1,0:T(8,128)S(1)} custom-call(s32[4]{0:T(128)S(1)} %copy-done.30, bf16[3,8,64,1024]{3,2,1,0:T(8,128)(2,1)S(1)} %get-tuple-element.30.acts, bf16[3,8,128,128]{3,2,1,0:T(8,128)(2,1)S(1)} %get-tuple-element.28.mixing), custom_call_target="tpu_custom_call" | custom-call | tf_op jit(solution)/shard_map/slope/pallas_call | solution.py:274
  18.0 0.6 chain.11
  18.6 0.5 collective-permute-start.5
  19.0 0.7 collective-permute-start.3
  19.7 0.6 chain.10
  20.3 1.1 %collective-permute-start.4 = (bf16[2,64,1024]{2,1,0:T(8,128)(2,1)S(1)}, bf16[2,64,1024]{2,1,0:T(8,128)(2,1)S(1)}, u32[]{:S(2)}, u32[]{:S(2)}) collective-permute-start(bf16[2,64,1024]{2,1,0:T(8,128)(2,1)S(1)} %get-tuple-element.34), channel_id=1, source_target_pairs={{0,4},{4,0},{8,12},{12,8},{1,5},{5,1},{9,13},{13,9},{2,6},{6,2},{1... | collective-permute-start | bytes 786440 | tf_op jit(solution)/shard_map/ppermute | solution.py:317
  21.8 4.1 %collective-permute-start.13 = (bf16[3,256,128]{2,1,0:T(8,128)(2,1)S(1)}, bf16[3,256,128]{2,1,0:T(8,128)(2,1)S(1)}, u32[]{:S(2)}, u32[]{:S(2)}) collective-permute-start(bf16[3,256,128]{2,1,0:T(8,128)(2,1)S(1)} %add_convert_fusion), channel_id=1, source_target_pairs={{0,2},{1,3},{2,0},{3,1},{4,6},{5,7},{6,4},{7,5},{8,10},{9,11},{10,... | collective-permute-start | bytes 589832 | tf_op jit(solution)/shard_map/ppermute | solution.py:241
  25.9 1.5 %slope.5.refs_1_ = f32[3,2,64,1024]{3,2,1,0:T(8,128)S(1)} custom-call(s32[4]{0:T(128)S(1)} %copy-done.30, bf16[3,8,64,1024]{3,2,1,0:T(8,128)(2,1)S(1)} %get-tuple-element.30.acts, bf16[3,8,128,128]{3,2,1,0:T(8,128)(2,1)S(1)} %get-tuple-element.28.mixing), custom_call_target="tpu_custom_call" | custom-call | tf_op jit(solution)/shard_map/slope/pallas_call | solution.py:274
  27.4 0.6 chain.13
  28.0 0.7 collective-permute-start.6
  28.7 1.5 %chain.12 = (bf16[2,64,1024]{2,1,0:T(8,128)(2,1)S(1)}, bf16[3,2,64,1024]{3,2,1,0:T(8,128)(2,1)S(1)}) custom-call(s32[4]{0:T(128)S(1)} %copy-done.30, bf16[3,8,128,128]{3,2,1,0:T(8,128)(2,1)S(1)} %get-tuple-element.28.mixing, bf16[2,64,1024]{2,1,0:T(8,128)(2,1)S(1)} %collective-permute-done.3.refs_0_, f32[3,2,64,1024]{3,2,1,0:T(8,128)S(1)} %slope.3.refs_1_.refs_3_, ...), custom_call_target="tpu_custom_call" | custom-call | tf_op jit(solution)/shard_map/chain/pallas_call | solution.py:274
  30.3 0.5 collective-permute-start.8
  30.8 4.3 %collective-permute-done.13 = bf16[3,256,128]{2,1,0:T(8,128)(2,1)S(1)} collective-permute-done((bf16[3,256,128]{2,1,0:T(8,128)(2,1)S(1)}, bf16[3,256,128]{2,1,0:T(8,128)(2,1)S(1)}, u32[]{:S(2)}, u32[]{:S(2)}) %collective-permute-start.13) | collective-permute-done | bytes 196640 | tf_op jit(solution)/shard_map/ppermute | solution.py:241
  35.2 1.5 %chain.14 = (bf16[2,64,1024]{2,1,0:T(8,128)(2,1)S(1)}, bf16[3,2,64,1024]{3,2,1,0:T(8,128)(2,1)S(1)}) custom-call(s32[4]{0:T(128)S(1)} %copy-done.30, bf16[3,8,128,128]{3,2,1,0:T(8,128)(2,1)S(1)} %get-tuple-element.28.mixing, bf16[2,64,1024]{2,1,0:T(8,128)(2,1)S(1)} %collective-permute-done.6.refs_0_, f32[3,2,64,1024]{3,2,1,0:T(8,128)S(1)} %slope.4.refs_1_.refs_3_, ...), custom_call_target="tpu_custom_call" | custom-call | tf_op jit(solution)/shard_map/chain/pallas_call | solution.py:274
  36.8 2.6 %sketch.2 = bf16[3,4,32,128]{3,2,1,0:T(8,128)(2,1)S(1)} custom-call(s32[4]{0:T(128)S(1)} %copy-done.30, bf16[3,2,64,1024]{3,2,1,0:T(8,128)(2,1)S(1)} %get-tuple-element.42.refs_0_, bf16[3,2,64,1024]{3,2,1,0:T(8,128)(2,1)S(1)} %get-tuple-element.43.refs_1_, bf16[3,2,64,1024]{3,2,1,0:T(8,128)(2,1)S(1)} %get-tuple-element.44.refs_2_.refs_0_, ...), custom_call_target="tpu_custom_call" | custom-call | tf_op jit(solution)/shard_map/sketch/pallas_call | solution.py:274
  39.4 1.6 %collective-permute-start.14 = (bf16[3,4,32,128]{3,2,1,0:T(8,128)(2,1)S(1)}, bf16[3,4,32,128]{3,2,1,0:T(8,128)(2,1)S(1)}, u32[]{:S(2)}, u32[]{:S(2)}) collective-permute-start(bf16[3,4,32,128]{3,2,1,0:T(8,128)(2,1)S(1)} %sketch.2), channel_id=1, source_target_pairs={{0,16},{16,0},{1,17},{17,1},{2,18},{18,2},{3,19},{19,3},{4,20},{20... | collective-permute-start | bytes 294920 | tf_op jit(solution)/shard_map/ppermute | solution.py:241
  40.9 0.6 chain.15
  41.5 0.7 collective-permute-start.9
  42.2 1.8 %collective-permute-done.14 = bf16[3,4,32,128]{3,2,1,0:T(8,128)(2,1)S(1)} collective-permute-done((bf16[3,4,32,128]{3,2,1,0:T(8,128)(2,1)S(1)}, bf16[3,4,32,128]{3,2,1,0:T(8,128)(2,1)S(1)}, u32[]{:S(2)}, u32[]{:S(2)}) %collective-permute-start.14) | collective-permute-done | bytes 98336 | tf_op jit(solution)/shard_map/ppermute | solution.py:241
  44.1 0.8 collective-permute-start.15
  44.9 2.4 %chain.16 = (bf16[2,64,1024]{2,1,0:T(8,128)(2,1)}, bf16[3,2,64,1024]{3,2,1,0:T(8,128)(2,1)S(1)}) custom-call(s32[4]{0:T(128)S(1)} %copy-done.30, bf16[3,8,128,128]{3,2,1,0:T(8,128)(2,1)S(1)} %get-tuple-element.28.mixing, bf16[2,64,1024]{2,1,0:T(8,128)(2,1)S(1)} %collective-permute-done.9.refs_0_, f32[3,2,64,1024]{3,2,1,0:T(8,128)S(1)} %slope.5.refs_1_, ...), custom_call_target="tpu_custom_call" | custom-call | tf_op jit(solution)/shard_map/chain/pallas_call | solution.py:274
  47.3 0.9 %copy-done.12 = bf16[3,2,64,1024]{3,2,1,0:T(8,128)(2,1)} copy-done((bf16[3,2,64,1024]{3,2,1,0:T(8,128)(2,1)}, bf16[3,2,64,1024]{3,2,1,0:T(8,128)(2,1)S(1)}, u32[]{:S(2)}) %copy-start.12) | copy-done | bytes 786456
  48.2 4.2 %collective-permute-start.11 = (bf16[2,64,1024]{2,1,0:T(8,128)(2,1)}, bf16[2,64,1024]{2,1,0:T(8,128)(2,1)}, u32[]{:S(2)}, u32[]{:S(2)}) collective-permute-start(bf16[2,64,1024]{2,1,0:T(8,128)(2,1)} %get-tuple-element.40), channel_id=1, source_target_pairs={{0,4},{4,0},{8,12},{12,8},{1,5},{5,1},{9,13},{13,9},{2,6},{6,2},{1... | collective-permute-start | bytes 786440 | tf_op jit(solution)/shard_map/ppermute | solution.py:317
  52.4 0.7 add_convert_fusion.3
  53.1 0.8 %collective-permute-done.11.refs_0_ = bf16[2,64,1024]{2,1,0:T(8,128)(2,1)} collective-permute-done((bf16[2,64,1024]{2,1,0:T(8,128)(2,1)}, bf16[2,64,1024]{2,1,0:T(8,128)(2,1)}, u32[]{:S(2)}, u32[]{:S(2)}) %collective-permute-start.11) | collective-permute-done | bytes 262176 | tf_op jit(solution)/shard_map/ppermute | solution.py:317
  53.9 1.9 %chain.17 = (bf16[2,64,1024]{2,1,0:T(8,128)(2,1)S(1)}, bf16[3,2,64,1024]{3,2,1,0:T(8,128)(2,1)S(1)}) custom-call(s32[4]{0:T(128)S(1)} %copy-done.31, bf16[3,8,128,128]{3,2,1,0:T(8,128)(2,1)S(1)} %get-tuple-element.28.mixing, bf16[2,64,1024]{2,1,0:T(8,128)(2,1)} %collective-permute-done.11.refs_0_, f32[3,2,64,1024]{3,2,1,0:T(8,128)S(1)} %slope.5.refs_1_), custom_call_target="tpu_custom_call" | custom-call | tf_op jit(solution)/shard_map/chain/pallas_call | solution.py:274
  55.9 1.1 %copy-done.11 = bf16[3,2,64,1024]{3,2,1,0:T(8,128)(2,1)S(1)} copy-done((bf16[3,2,64,1024]{3,2,1,0:T(8,128)(2,1)S(1)}, bf16[3,2,64,1024]{3,2,1,0:T(8,128)(2,1)}, u32[]{:S(2)}) %copy-start.11) | copy-done | bytes 786456
  57.0 1.1 %copy-done.13 = bf16[3,2,64,1024]{3,2,1,0:T(8,128)(2,1)S(1)} copy-done((bf16[3,2,64,1024]{3,2,1,0:T(8,128)(2,1)S(1)}, bf16[3,2,64,1024]{3,2,1,0:T(8,128)(2,1)}, u32[]{:S(2)}) %copy-start.13) | copy-done | bytes 786456
  58.2 2.6 %sketch.3 = bf16[3,4,32,128]{3,2,1,0:T(8,128)(2,1)S(1)} custom-call(s32[4]{0:T(128)S(1)} %copy-done.31, bf16[3,2,64,1024]{3,2,1,0:T(8,128)(2,1)S(1)} %get-tuple-element.44.refs_2_.refs_0_, bf16[3,2,64,1024]{3,2,1,0:T(8,128)(2,1)S(1)} %copy-done.9, bf16[3,2,64,1024]{3,2,1,0:T(8,128)(2,1)S(1)} %copy-done.11, bf16[3,2,64,1024]{3,2,1,0:T(8,128)(2,1)S(1)} %copy-done.2, ...), custom_call_target="tpu_custom_call" | custom-call | tf_op jit(solution)/shard_map/sketch/pallas_call | solution.py:274
  60.8 0.7 collective-permute-start.17
  61.5 1.0 %convert_add_fusion.2 = f32[3,4,32,128]{3,2,1,0:T(8,128)S(1)} fusion(bf16[3,4,32,128]{3,2,1,0:T(8,128)(2,1)} %collective-permute-done.16, bf16[3,4,32,128]{3,2,1,0:T(8,128)(2,1)} %add_convert_fusion.3), kind=kLoop, calls=%fused_computation.14 | loop fusion | flops 147456 | bytes 393216 | tf_op jit(solution)/shard_map/add | solution.py:242
  62.5 3.0 %collective-permute-done.17 = bf16[3,4,32,128]{3,2,1,0:T(8,128)(2,1)S(1)} collective-permute-done((bf16[3,4,32,128]{3,2,1,0:T(8,128)(2,1)S(1)}, bf16[3,4,32,128]{3,2,1,0:T(8,128)(2,1)S(1)}, u32[]{:S(2)}, u32[]{:S(2)}) %collective-permute-start.17) | collective-permute-done | bytes 98336 | tf_op jit(solution)/shard_map/ppermute | solution.py:241
  65.5 3.5 %collective-permute-start.18 = (bf16[3,4,32,128]{3,2,1,0:T(8,128)(2,1)S(1)}, bf16[3,4,32,128]{3,2,1,0:T(8,128)(2,1)S(1)}, u32[]{:S(2)}, u32[]{:S(2)}) collective-permute-start(bf16[3,4,32,128]{3,2,1,0:T(8,128)(2,1)S(1)} %add_convert_fusion.2), channel_id=1, source_target_pairs={{0,1},{1,0},{2,3},{3,2},{4,5},{5,4},{6,7},{7,6},{8,9},{9,8},{10,11... | collective-permute-start | bytes 294920 | tf_op jit(solution)/shard_map/ppermute | solution.py:241
  69.0 1.1 %select_select_fusion.1 = (bf16[2,64,1024]{2,1,0:T(8,128)(2,1)S(1)}, bf16[2,64,1024]{2,1,0:T(8,128)(2,1)S(1)}, bf16[2,64,1024]{2,1,0:T(8,128)(2,1)S(1)}, bf16[2,64,1024]{2,1,0:T(8,128)(2,1)S(1)}) fusion(bf16[2,64,1024]{2,1,0:T(8,128)(2,1)S(1)} %copy-done.21, bf16[2,64,1024]{2,1,0:T(8,128)(2,1)S(1)} %copy-done.15, pred[]{:T(512)S(6)} %eq.10, pred[]{:T(512)S(6)} %eq.9, ...), kind=kLoop, calls=%fused_computation.5 | loop fusion | flops 1179648 | bytes 3670018 | tf_op jit(solution)/shard_map/jit(_where)/select_n | solution.py:367
  70.1 2.5 %collective-permute-done.18 = bf16[3,4,32,128]{3,2,1,0:T(8,128)(2,1)S(1)} collective-permute-done((bf16[3,4,32,128]{3,2,1,0:T(8,128)(2,1)S(1)}, bf16[3,4,32,128]{3,2,1,0:T(8,128)(2,1)S(1)}, u32[]{:S(2)}, u32[]{:S(2)}) %collective-permute-start.18) | collective-permute-done | bytes 98336 | tf_op jit(solution)/shard_map/ppermute | solution.py:241
  72.7 1.1 %maximum_bitcast_fusion = bf16[1,8,64,1024]{3,2,1,0:T(8,128)(2,1)} fusion(bf16[2,64,1024]{2,1,0:T(8,128)(2,1)S(1)} %get-tuple-element.57, bf16[2,64,1024]{2,1,0:T(8,128)(2,1)S(1)} %get-tuple-element.56, bf16[2,64,1024]{2,1,0:T(8,128)(2,1)S(1)} %get-tuple-element.55, bf16[2,64,1024]{2,1,0:T(8,128)(2,1)S(1)} %get-tuple-element.54), kind=kLoop, calls=%fused_computation | loop fusion | flops 1572864 | bytes 2097152 | tf_op jit(solution)/shard_map/broadcast_in_dim | solution.py:368
  73.8 5.5 %collective-permute-done.19 = bf16[3,4,32,128]{3,2,1,0:T(8,128)(2,1)S(1)} collective-permute-done((bf16[3,4,32,128]{3,2,1,0:T(8,128)(2,1)S(1)}, bf16[3,4,32,128]{3,2,1,0:T(8,128)(2,1)S(1)}, u32[]{:S(2)}, u32[]{:S(2)}) %collective-permute-start.19) | collective-permute-done | bytes 98336 | tf_op jit(solution)/shard_map/ppermute | solution.py:241
  79.4 0.8 %broadcast_in_dim_reshape.3 = f32[1,3,8,4096]{3,2,1,0:T(8,128)} reshape(f32[3,8,32,128]{3,2,1,0:T(8,128)S(1)} %pad_maximum_fusion) | data formatting | bytes 786432 | tf_op jit(solution)/shard_map/broadcast_in_dim;reshape | solution.py:368
  (87 shorter events, 1.1 us)
Async XLA Ops:
  0.6 1.9 %copy-start = (bf16[1,3,8,64,1024]{4,3,2,1,0:T(8,128)(2,1)S(1)}, bf16[1,3,8,64,1024]{4,3,2,1,0:T(8,128)(2,1)}, u32[]{:S(2)}) copy-start(bf16[1,3,8,64,1024]{4,3,2,1,0:T(8,128)(2,1)} %param.7) | copy-start | bytes 9437188
  2.5 1.2 %copy-start.5 = (bf16[8,64,1024]{2,1,0:T(8,128)(2,1)S(1)}, bf16[8,64,1024]{2,1,0:T(8,128)(2,1)}, u32[]{:S(2)}) copy-start(bf16[8,64,1024]{2,1,0:T(8,128)(2,1)} %top.1) | copy-start | bytes 3145732
  7.5 1.6 %copy-start.14 = (bf16[2,64,1024]{2,1,0:T(8,128)(2,1)}, bf16[2,64,1024]{2,1,0:T(8,128)(2,1)S(1)}, u32[]{:S(2)}) copy-start(bf16[2,64,1024]{2,1,0:T(8,128)(2,1)S(1)} %get-tuple-element.31) | copy-start | bytes 786436
  7.5 1.6 %collective-permute-start = (bf16[2,64,1024]{2,1,0:T(8,128)(2,1)S(1)}, bf16[2,64,1024]{2,1,0:T(8,128)(2,1)S(1)}, u32[]{:S(2)}, u32[]{:S(2)}) collective-permute-start(bf16[2,64,1024]{2,1,0:T(8,128)(2,1)S(1)} %get-tuple-element.31), channel_id=1, source_target_pairs={{0,4},{4,0},{8,12},{12,8},{1,5},{5,1},{9,13},{13,9},{2,6},{6,2},{1... | collective-permute-start | bytes 786440 | tf_op jit(solution)/shard_map/ppermute | solution.py:317
  9.1 1.5 %copy-start.32 = (s32[1,3,8]{2,0,1:T(1,128)S(1)}, s32[1,3,8]{2,0,1:T(1,128)}, u32[]{:S(2)}) copy-start(s32[1,3,8]{2,0,1:T(1,128)} %param.10) | copy-start | bytes 292
  9.1 1.5 %copy-start.7 = (bf16[1,3,8,128,128]{4,3,2,1,0:T(8,128)(2,1)S(1)}, bf16[1,3,8,128,128]{4,3,2,1,0:T(8,128)(2,1)}, u32[]{:S(2)}) copy-start(bf16[1,3,8,128,128]{4,3,2,1,0:T(8,128)(2,1)} %param.9) | copy-start | bytes 2359300
  9.7 3.8 %copy-start.16 = (bf16[2,64,1024]{2,1,0:T(8,128)(2,1)}, bf16[2,64,1024]{2,1,0:T(8,128)(2,1)S(1)}, u32[]{:S(2)}) copy-start(bf16[2,64,1024]{2,1,0:T(8,128)(2,1)S(1)} %get-tuple-element.33) | copy-start | bytes 786436
  9.7 8.3 %collective-permute-start.2 = (bf16[2,64,1024]{2,1,0:T(8,128)(2,1)S(1)}, bf16[2,64,1024]{2,1,0:T(8,128)(2,1)S(1)}, u32[]{:S(2)}, u32[]{:S(2)}) collective-permute-start(bf16[2,64,1024]{2,1,0:T(8,128)(2,1)S(1)} %get-tuple-element.33), channel_id=1, source_target_pairs={{0,4},{4,0},{8,12},{12,8},{1,5},{5,1},{9,13},{13,9},{2,6},{6,2},{1... | collective-permute-start | bytes 786440 | tf_op jit(solution)/shard_map/ppermute | solution.py:317
  9.9 9.8 %collective-permute-start.1 = (bf16[2,64,1024]{2,1,0:T(8,128)(2,1)S(1)}, bf16[2,64,1024]{2,1,0:T(8,128)(2,1)S(1)}, u32[]{:S(2)}, u32[]{:S(2)}) collective-permute-start(bf16[2,64,1024]{2,1,0:T(8,128)(2,1)S(1)} %get-tuple-element.33), channel_id=1, source_target_pairs={{8,4},{9,5},{10,6},{11,7},{24,20},{25,21},{26,22},{27,23}} | collective-permute-start | bytes 786440 | tf_op jit(solution)/shard_map/ppermute | solution.py:320
  13.5 23.2 %copy-start.3 = (bf16[3,64,1024]{2,1,0:T(8,128)(2,1)}, bf16[3,64,1024]{2,1,0:T(8,128)(2,1)S(1)}, u32[]{:S(2)}) copy-start(bf16[3,64,1024]{2,1,0:T(8,128)(2,1)S(1)} %get-tuple-element.48.refs_6_) | copy-start | bytes 1179652
  13.6 8.1 %collective-permute-start.12 = (bf16[3,256,128]{2,1,0:T(8,128)(2,1)S(1)}, bf16[3,256,128]{2,1,0:T(8,128)(2,1)S(1)}, u32[]{:S(2)}, u32[]{:S(2)}) collective-permute-start(bf16[3,256,128]{2,1,0:T(8,128)(2,1)S(1)} %get-tuple-element.49), channel_id=1, source_target_pairs={{0,1},{1,0},{2,3},{3,2},{4,5},{5,4},{6,7},{7,6},{8,9},{9,8},{10,11... | collective-permute-start | bytes 589832 | tf_op jit(solution)/shard_map/ppermute | solution.py:241
  18.6 3.2 %copy-start.18 = (bf16[2,64,1024]{2,1,0:T(8,128)(2,1)}, bf16[2,64,1024]{2,1,0:T(8,128)(2,1)S(1)}, u32[]{:S(2)}) copy-start(bf16[2,64,1024]{2,1,0:T(8,128)(2,1)S(1)} %get-tuple-element.35) | copy-start | bytes 786436
  18.6 8.8 %collective-permute-start.5 = (bf16[2,64,1024]{2,1,0:T(8,128)(2,1)S(1)}, bf16[2,64,1024]{2,1,0:T(8,128)(2,1)S(1)}, u32[]{:S(2)}, u32[]{:S(2)}) collective-permute-start(bf16[2,64,1024]{2,1,0:T(8,128)(2,1)S(1)} %get-tuple-element.35), channel_id=1, source_target_pairs={{0,4},{4,0},{8,12},{12,8},{1,5},{5,1},{9,13},{13,9},{2,6},{6,2},{1... | collective-permute-start | bytes 786440 | tf_op jit(solution)/shard_map/ppermute | solution.py:317
  19.0 9.6 %collective-permute-start.3 = (bf16[2,64,1024]{2,1,0:T(8,128)(2,1)S(1)}, bf16[2,64,1024]{2,1,0:T(8,128)(2,1)S(1)}, u32[]{:S(2)}, u32[]{:S(2)}) collective-permute-start(bf16[2,64,1024]{2,1,0:T(8,128)(2,1)S(1)} %get-tuple-element.35), channel_id=1, source_target_pairs={{8,4},{9,5},{10,6},{11,7},{24,20},{25,21},{26,22},{27,23}} | collective-permute-start | bytes 786440 | tf_op jit(solution)/shard_map/ppermute | solution.py:320
  20.3 7.1 %copy-start.20 = (bf16[2,64,1024]{2,1,0:T(8,128)(2,1)}, bf16[2,64,1024]{2,1,0:T(8,128)(2,1)S(1)}, u32[]{:S(2)}) copy-start(bf16[2,64,1024]{2,1,0:T(8,128)(2,1)S(1)} %get-tuple-element.34) | copy-start | bytes 786436
  20.3 8.4 %collective-permute-start.4 = (bf16[2,64,1024]{2,1,0:T(8,128)(2,1)S(1)}, bf16[2,64,1024]{2,1,0:T(8,128)(2,1)S(1)}, u32[]{:S(2)}, u32[]{:S(2)}) collective-permute-start(bf16[2,64,1024]{2,1,0:T(8,128)(2,1)S(1)} %get-tuple-element.34), channel_id=1, source_target_pairs={{0,4},{4,0},{8,12},{12,8},{1,5},{5,1},{9,13},{13,9},{2,6},{6,2},{1... | collective-permute-start | bytes 786440 | tf_op jit(solution)/shard_map/ppermute | solution.py:317
  21.8 13.4 %collective-permute-start.13 = (bf16[3,256,128]{2,1,0:T(8,128)(2,1)S(1)}, bf16[3,256,128]{2,1,0:T(8,128)(2,1)S(1)}, u32[]{:S(2)}, u32[]{:S(2)}) collective-permute-start(bf16[3,256,128]{2,1,0:T(8,128)(2,1)S(1)} %add_convert_fusion), channel_id=1, source_target_pairs={{0,2},{1,3},{2,0},{3,1},{4,6},{5,7},{6,4},{7,5},{8,10},{9,11},{10,... | collective-permute-start | bytes 589832 | tf_op jit(solution)/shard_map/ppermute | solution.py:241
  28.0 2.2 %copy-start.8 = (bf16[3,2,64,1024]{3,2,1,0:T(8,128)(2,1)}, bf16[3,2,64,1024]{3,2,1,0:T(8,128)(2,1)S(1)}, u32[]{:S(2)}) copy-start(bf16[3,2,64,1024]{3,2,1,0:T(8,128)(2,1)S(1)} %get-tuple-element.50.refs_1_) | copy-start | bytes 2359300
  28.0 2.3 %copy-start.22 = (bf16[2,64,1024]{2,1,0:T(8,128)(2,1)}, bf16[2,64,1024]{2,1,0:T(8,128)(2,1)S(1)}, u32[]{:S(2)}) copy-start(bf16[2,64,1024]{2,1,0:T(8,128)(2,1)S(1)} %get-tuple-element.37) | copy-start | bytes 786436
  28.0 7.2 %collective-permute-start.6 = (bf16[2,64,1024]{2,1,0:T(8,128)(2,1)S(1)}, bf16[2,64,1024]{2,1,0:T(8,128)(2,1)S(1)}, u32[]{:S(2)}, u32[]{:S(2)}) collective-permute-start(bf16[2,64,1024]{2,1,0:T(8,128)(2,1)S(1)} %get-tuple-element.37), channel_id=1, source_target_pairs={{8,4},{9,5},{10,6},{11,7},{24,20},{25,21},{26,22},{27,23}} | collective-permute-start | bytes 786440 | tf_op jit(solution)/shard_map/ppermute | solution.py:320
  30.2 6.5 %copy-start.24 = (bf16[2,64,1024]{2,1,0:T(8,128)(2,1)}, bf16[2,64,1024]{2,1,0:T(8,128)(2,1)S(1)}, u32[]{:S(2)}) copy-start(bf16[2,64,1024]{2,1,0:T(8,128)(2,1)S(1)} %get-tuple-element.36) | copy-start | bytes 786436
  30.2 5.0 %collective-permute-start.7 = (bf16[2,64,1024]{2,1,0:T(8,128)(2,1)S(1)}, bf16[2,64,1024]{2,1,0:T(8,128)(2,1)S(1)}, u32[]{:S(2)}, u32[]{:S(2)}) collective-permute-start(bf16[2,64,1024]{2,1,0:T(8,128)(2,1)S(1)} %get-tuple-element.36), channel_id=1, source_target_pairs={{0,4},{4,0},{8,12},{12,8},{1,5},{5,1},{9,13},{13,9},{2,6},{6,2},{1... | collective-permute-start | bytes 786440 | tf_op jit(solution)/shard_map/ppermute | solution.py:317
  30.3 10.6 %collective-permute-start.8 = (bf16[2,64,1024]{2,1,0:T(8,128)(2,1)S(1)}, bf16[2,64,1024]{2,1,0:T(8,128)(2,1)S(1)}, u32[]{:S(2)}, u32[]{:S(2)}) collective-permute-start(bf16[2,64,1024]{2,1,0:T(8,128)(2,1)S(1)} %get-tuple-element.37), channel_id=1, source_target_pairs={{0,4},{4,0},{8,12},{12,8},{1,5},{5,1},{9,13},{13,9},{2,6},{6,2},{1... | collective-permute-start | bytes 786440 | tf_op jit(solution)/shard_map/ppermute | solution.py:317
  36.7 2.6 %copy-start.1 = (bf16[3,2,64,1024]{3,2,1,0:T(8,128)(2,1)}, bf16[3,2,64,1024]{3,2,1,0:T(8,128)(2,1)S(1)}, u32[]{:S(2)}) copy-start(bf16[3,2,64,1024]{3,2,1,0:T(8,128)(2,1)S(1)} %get-tuple-element.47.refs_5_.refs_3_) | copy-start | bytes 2359300
  36.7 4.2 %copy-start.26 = (bf16[2,64,1024]{2,1,0:T(8,128)(2,1)}, bf16[2,64,1024]{2,1,0:T(8,128)(2,1)S(1)}, u32[]{:S(2)}) copy-start(bf16[2,64,1024]{2,1,0:T(8,128)(2,1)S(1)} %get-tuple-element.38) | copy-start | bytes 786436
  39.4 4.7 %collective-permute-start.14 = (bf16[3,4,32,128]{3,2,1,0:T(8,128)(2,1)S(1)}, bf16[3,4,32,128]{3,2,1,0:T(8,128)(2,1)S(1)}, u32[]{:S(2)}, u32[]{:S(2)}) collective-permute-start(bf16[3,4,32,128]{3,2,1,0:T(8,128)(2,1)S(1)} %sketch.2), channel_id=1, source_target_pairs={{0,16},{16,0},{1,17},{17,1},{2,18},{18,2},{3,19},{19,3},{4,20},{20... | collective-permute-start | bytes 294920 | tf_op jit(solution)/shard_map/ppermute | solution.py:241
  40.9 3.9 %collective-permute-start.10 = (bf16[2,64,1024]{2,1,0:T(8,128)(2,1)S(1)}, bf16[2,64,1024]{2,1,0:T(8,128)(2,1)S(1)}, u32[]{:S(2)}, u32[]{:S(2)}) collective-permute-start(bf16[2,64,1024]{2,1,0:T(8,128)(2,1)S(1)} %get-tuple-element.38), channel_id=1, source_target_pairs={{0,4},{4,0},{8,12},{12,8},{1,5},{5,1},{9,13},{13,9},{2,6},{6,2},{1... | collective-permute-start | bytes 786440 | tf_op jit(solution)/shard_map/ppermute | solution.py:317
  41.5 5.8 %copy-start.10 = (bf16[3,2,64,1024]{3,2,1,0:T(8,128)(2,1)}, bf16[3,2,64,1024]{3,2,1,0:T(8,128)(2,1)S(1)}, u32[]{:S(2)}) copy-start(bf16[3,2,64,1024]{3,2,1,0:T(8,128)(2,1)S(1)} %get-tuple-element.51.refs_2_) | copy-start | bytes 2359300
  41.5 5.8 %copy-start.28 = (bf16[2,64,1024]{2,1,0:T(8,128)(2,1)}, bf16[2,64,1024]{2,1,0:T(8,128)(2,1)S(1)}, u32[]{:S(2)}) copy-start(bf16[2,64,1024]{2,1,0:T(8,128)(2,1)S(1)} %get-tuple-element.39) | copy-start | bytes 786436
  41.5 3.3 %collective-permute-start.9 = (bf16[2,64,1024]{2,1,0:T(8,128)(2,1)S(1)}, bf16[2,64,1024]{2,1,0:T(8,128)(2,1)S(1)}, u32[]{:S(2)}, u32[]{:S(2)}) collective-permute-start(bf16[2,64,1024]{2,1,0:T(8,128)(2,1)S(1)} %get-tuple-element.39), channel_id=1, source_target_pairs={{8,4},{9,5},{10,6},{11,7},{24,20},{25,21},{26,22},{27,23}} | collective-permute-start | bytes 786440 | tf_op jit(solution)/shard_map/ppermute | solution.py:320
  44.1 9.8 %copy-start.31 = (s32[4]{0:T(128)S(1)}, s32[4]{0:T(128)}, u32[]{:S(2)}) copy-start(s32[4]{0:T(128)} %sizes.29) | copy-start | bytes 52
  44.1 8.3 %collective-permute-start.15 = (bf16[3,4,32,128]{3,2,1,0:T(8,128)(2,1)S(1)}, bf16[3,4,32,128]{3,2,1,0:T(8,128)(2,1)S(1)}, u32[]{:S(2)}, u32[]{:S(2)}) collective-permute-start(bf16[3,4,32,128]{3,2,1,0:T(8,128)(2,1)S(1)} %add_convert_fusion.4), channel_id=1, source_target_pairs={{0,1},{1,0},{2,3},{3,2},{4,5},{5,4},{6,7},{7,6},{8,9},{9,8},{10,11... | collective-permute-start | bytes 294920 | tf_op jit(solution)/shard_map/ppermute | solution.py:241
  48.2 5.7 %collective-permute-start.11 = (bf16[2,64,1024]{2,1,0:T(8,128)(2,1)}, bf16[2,64,1024]{2,1,0:T(8,128)(2,1)}, u32[]{:S(2)}, u32[]{:S(2)}) collective-permute-start(bf16[2,64,1024]{2,1,0:T(8,128)(2,1)} %get-tuple-element.40), channel_id=1, source_target_pairs={{0,4},{4,0},{8,12},{12,8},{1,5},{5,1},{9,13},{13,9},{2,6},{6,2},{1... | collective-permute-start | bytes 786440 | tf_op jit(solution)/shard_map/ppermute | solution.py:317
  53.1 8.4 %collective-permute-start.16 = (bf16[3,4,32,128]{3,2,1,0:T(8,128)(2,1)}, bf16[3,4,32,128]{3,2,1,0:T(8,128)(2,1)}, u32[]{:S(2)}, u32[]{:S(2)}) collective-permute-start(bf16[3,4,32,128]{3,2,1,0:T(8,128)(2,1)} %add_convert_fusion.3), channel_id=1, source_target_pairs={{0,2},{1,3},{2,0},{3,1},{4,6},{5,7},{6,4},{7,5},{8,10},{9,11},{10,... | collective-permute-start | bytes 294920 | tf_op jit(solution)/shard_map/ppermute | solution.py:241
  53.1 2.8 %copy-start.2 = (bf16[3,2,64,1024]{3,2,1,0:T(8,128)(2,1)S(1)}, bf16[3,2,64,1024]{3,2,1,0:T(8,128)(2,1)}, u32[]{:S(2)}) copy-start(bf16[3,2,64,1024]{3,2,1,0:T(8,128)(2,1)} %copy-done.1) | copy-start | bytes 2359300
  53.1 2.8 %copy-start.4 = (bf16[3,64,1024]{2,1,0:T(8,128)(2,1)S(1)}, bf16[3,64,1024]{2,1,0:T(8,128)(2,1)}, u32[]{:S(2)}) copy-start(bf16[3,64,1024]{2,1,0:T(8,128)(2,1)} %copy-done.3) | copy-start | bytes 1179652
  53.1 2.8 %copy-start.9 = (bf16[3,2,64,1024]{3,2,1,0:T(8,128)(2,1)S(1)}, bf16[3,2,64,1024]{3,2,1,0:T(8,128)(2,1)}, u32[]{:S(2)}) copy-start(bf16[3,2,64,1024]{3,2,1,0:T(8,128)(2,1)} %copy-done.8) | copy-start | bytes 2359300
  58.1 10.8 %copy-start.15 = (bf16[2,64,1024]{2,1,0:T(8,128)(2,1)S(1)}, bf16[2,64,1024]{2,1,0:T(8,128)(2,1)}, u32[]{:S(2)}) copy-start(bf16[2,64,1024]{2,1,0:T(8,128)(2,1)} %copy-done.14) | copy-start | bytes 786436
  58.1 10.8 %copy-start.17 = (bf16[2,64,1024]{2,1,0:T(8,128)(2,1)S(1)}, bf16[2,64,1024]{2,1,0:T(8,128)(2,1)}, u32[]{:S(2)}) copy-start(bf16[2,64,1024]{2,1,0:T(8,128)(2,1)} %copy-done.16) | copy-start | bytes 786436
  58.1 10.8 %copy-start.19 = (bf16[2,64,1024]{2,1,0:T(8,128)(2,1)S(1)}, bf16[2,64,1024]{2,1,0:T(8,128)(2,1)}, u32[]{:S(2)}) copy-start(bf16[2,64,1024]{2,1,0:T(8,128)(2,1)} %copy-done.18) | copy-start | bytes 786436
  58.1 10.8 %copy-start.21 = (bf16[2,64,1024]{2,1,0:T(8,128)(2,1)S(1)}, bf16[2,64,1024]{2,1,0:T(8,128)(2,1)}, u32[]{:S(2)}) copy-start(bf16[2,64,1024]{2,1,0:T(8,128)(2,1)} %copy-done.20) | copy-start | bytes 786436
  58.2 10.8 %copy-start.23 = (bf16[2,64,1024]{2,1,0:T(8,128)(2,1)S(1)}, bf16[2,64,1024]{2,1,0:T(8,128)(2,1)}, u32[]{:S(2)}) copy-start(bf16[2,64,1024]{2,1,0:T(8,128)(2,1)} %copy-done.22) | copy-start | bytes 786436
  58.2 10.8 %copy-start.25 = (bf16[2,64,1024]{2,1,0:T(8,128)(2,1)S(1)}, bf16[2,64,1024]{2,1,0:T(8,128)(2,1)}, u32[]{:S(2)}) copy-start(bf16[2,64,1024]{2,1,0:T(8,128)(2,1)} %copy-done.24) | copy-start | bytes 786436
  58.2 10.8 %copy-start.27 = (bf16[2,64,1024]{2,1,0:T(8,128)(2,1)S(1)}, bf16[2,64,1024]{2,1,0:T(8,128)(2,1)}, u32[]{:S(2)}) copy-start(bf16[2,64,1024]{2,1,0:T(8,128)(2,1)} %copy-done.26) | copy-start | bytes 786436
  58.2 10.8 %copy-start.29 = (bf16[2,64,1024]{2,1,0:T(8,128)(2,1)S(1)}, bf16[2,64,1024]{2,1,0:T(8,128)(2,1)}, u32[]{:S(2)}) copy-start(bf16[2,64,1024]{2,1,0:T(8,128)(2,1)} %copy-done.28) | copy-start | bytes 786436
  60.8 4.7 %collective-permute-start.17 = (bf16[3,4,32,128]{3,2,1,0:T(8,128)(2,1)S(1)}, bf16[3,4,32,128]{3,2,1,0:T(8,128)(2,1)S(1)}, u32[]{:S(2)}, u32[]{:S(2)}) collective-permute-start(bf16[3,4,32,128]{3,2,1,0:T(8,128)(2,1)S(1)} %sketch.3), channel_id=1, source_target_pairs={{0,16},{16,0},{1,17},{17,1},{2,18},{18,2},{3,19},{19,3},{4,20},{20... | collective-permute-start | bytes 294920 | tf_op jit(solution)/shard_map/ppermute | solution.py:241
  65.5 7.1 %collective-permute-start.18 = (bf16[3,4,32,128]{3,2,1,0:T(8,128)(2,1)S(1)}, bf16[3,4,32,128]{3,2,1,0:T(8,128)(2,1)S(1)}, u32[]{:S(2)}, u32[]{:S(2)}) collective-permute-start(bf16[3,4,32,128]{3,2,1,0:T(8,128)(2,1)S(1)} %add_convert_fusion.2), channel_id=1, source_target_pairs={{0,1},{1,0},{2,3},{3,2},{4,5},{5,4},{6,7},{7,6},{8,9},{9,8},{10,11... | collective-permute-start | bytes 294920 | tf_op jit(solution)/shard_map/ppermute | solution.py:241
  72.7 6.6 %collective-permute-start.19 = (bf16[3,4,32,128]{3,2,1,0:T(8,128)(2,1)S(1)}, bf16[3,4,32,128]{3,2,1,0:T(8,128)(2,1)S(1)}, u32[]{:S(2)}, u32[]{:S(2)}) collective-permute-start(bf16[3,4,32,128]{3,2,1,0:T(8,128)(2,1)S(1)} %add_convert_fusion.1), channel_id=1, source_target_pairs={{0,2},{1,3},{2,0},{3,1},{4,6},{5,7},{6,4},{7,5},{8,10},{9,11},{10,... | collective-permute-start | bytes 294920 | tf_op jit(solution)/shard_map/ppermute | solution.py:241
  (5 other events, 4.9 us)
